TPU v7x, 256 devices: a whole 4x4x8 slice. The times are simulated.
256 devices in a mesh: ctx: 16 (over x_lo, z), head: 2 (over core), ep: 8 (over y, x_hi).
Axes of the slice: x: 4 (x_hi: 2, x_lo: 2; x = x_hi * 2 + x_lo), y: 4, z: 8, core: 2. Of those that a mesh axis runs over, the one named last changes fastest.
Arguments:
- q_latent: bfloat16 [8192, 16, 576], P('ctx', ('head', 'ep')), may hold values from -20 to 20
- kv_latent: bfloat16 [8192, 576], P('ctx'), may hold values from -20 to 20
- w_value: bfloat16 [16, 512, 128], P(('head', 'ep')), may hold values from -0.25 to 0.25
- w_out: bfloat16 [2048, 2048], P(('head', 'ep')), may hold values from -0.125 to 0.125
- resid: bfloat16 [8192, 2048], P(('ctx', 'head', 'ep')), may hold values from -40 to 40
- norm_gain: float32 [2048], replicated, may hold values from 0.1 to 1.9
- w_gate: bfloat16 [16, 2048, 1408], P('ctx', None, 'head'), may hold values from -0.125 to 0.125
- w_up: bfloat16 [16, 2048, 1408], P('ctx', None, 'head'), may hold values from -0.125 to 0.125
- w_down_t: bfloat16 [16, 2048, 1408], P('ctx', None, 'head'), may hold values from -0.15625 to 0.15625
- expert_ids: int32 [8192, 6], P(('ctx', 'head', 'ep')), may hold values from 0 to 15, all different within a row; in each aligned block of 32 rows (0 to 31, 32 to 63, ...) at most 15 rows name the same one
- route_scores: float32 [8192, 6], P(('ctx', 'head', 'ep')), may hold values from 0.1 to 1
Outputs:
- layer_out: bfloat16 [8192, 2048], P(('ctx', 'head', 'ep'))
Inputs may be any that keep to these rules, and one draw needn't show every extreme that they name: `expert_ids`: each row names 6 different experts. In each aligned block of 32 rows (the rows of one device) no expert is named by more than 15 rows, and in some block an expert is named by exactly 15 rows.
All inputs are finite; a program needn't handle non-finite values.
Results may differ from a plain program's by a relative error of at most 0.007.
Values may be sent and summed in bfloat16 or wider, within the bound.
A program may use at most 128 MiB of HBM per device.

v0:
```python
import jax
import jax.numpy as jnp
from jax import lax
from jax.sharding import PartitionSpec as P

ROPE = 64
NOPE = 128
TOPK = 6


routed_factor = 2.446
norm_epsilon = 1e-06
masked_score = -1e30


def expert_half(inputs, gate_part, up_part, down_part):
    gate = jnp.dot(inputs, gate_part, preferred_element_type=jnp.float32)
    upward = jnp.dot(inputs, up_part, preferred_element_type=jnp.float32)
    hidden = (jax.nn.silu(gate) * upward).astype(jnp.bfloat16)
    return lax.dot_general(
        hidden, down_part, (((1,), (1,)), ((), ())), preferred_element_type=jnp.float32
    )


def make_projection(source, piece):
    return jnp.dot(source, piece, preferred_element_type=jnp.float32)


def per_device(
    q_latent,
    kv_latent,
    w_value,
    w_out,
    resid,
    norm_gain,
    w_gate,
    w_up,
    w_down_t,
    expert_ids,
    route_scores,
):
    tokens_here = q_latent.shape[0]
    heads_here = q_latent.shape[1]
    latent_width = w_value.shape[1]
    width = resid.shape[1]
    rows = resid.shape[0]
    query_rows = tokens_here * heads_here
    score_scale = (NOPE + ROPE) ** (-0.5)
    queries = q_latent.reshape(query_rows, q_latent.shape[2])
    first_token = lax.axis_index("ctx") * tokens_here
    last_token = first_token + tokens_here - 1
    query_pos = first_token + jnp.arange(query_rows, dtype=jnp.int32) // heads_here
    start_state = (
        jnp.full((query_rows,), masked_score, jnp.float32),
        jnp.zeros((query_rows,), jnp.float32),
        jnp.zeros((query_rows, latent_width), jnp.float32),
    )
    keys = lax.all_gather(kv_latent, "ctx", axis=0, tiled=True)
    count = keys.shape[0]

    def compute(state):
        highest, denominator, accum = state
        scores = (
            lax.dot_general(
                queries, keys, (((1,), (1,)), ((), ())), preferred_element_type=jnp.float32
            )
            * score_scale
        )
        key_pos = jnp.arange(count, dtype=jnp.int32)
        visible = key_pos[None, :] <= query_pos[:, None]
        scores = jnp.where(visible, scores, masked_score)
        new_highest = jnp.maximum(highest, jnp.max(scores, axis=1))
        weights = jnp.where(visible, jnp.exp(scores - new_highest[:, None]), 0.0)
        denominator = jnp.sum(weights, axis=1)
        values = keys[:, :latent_width]
        accum = jnp.dot(weights.astype(jnp.bfloat16), values, preferred_element_type=jnp.float32)
        return (new_highest, denominator, accum)

    highest, denominator, accum = lax.cond(
        jnp.int32(0) > last_token, lambda state: state, compute, start_state
    )
    latent_out = (
        (accum / denominator[:, None])
        .astype(jnp.bfloat16)
        .reshape(tokens_here, heads_here, latent_width)
    )
    head_out = jnp.einsum(
        "thl,hlv->thv", latent_out, w_value, preferred_element_type=jnp.float32
    ).astype(jnp.bfloat16)
    grouped = lax.all_to_all(head_out, ("head", "ep"), split_axis=0, concat_axis=1, tiled=True)
    flat_heads = grouped.reshape(rows, grouped.shape[1] * grouped.shape[2])
    attended = make_projection(
        flat_heads, lax.all_gather(w_out, ("head", "ep"), axis=0, tiled=True)
    )
    after_attn = lax.optimization_barrier(
        (resid.astype(jnp.float32) + attended).astype(jnp.bfloat16)
    )
    widened = after_attn.astype(jnp.float32)
    mean_square = jnp.mean(widened * widened, axis=1, keepdims=True)
    normed = (widened * lax.rsqrt(mean_square + norm_epsilon) * norm_gain).astype(jnp.bfloat16)
    experts_here = lax.axis_size("ctx")
    capacity = 5 * rows * TOPK // (4 * experts_here)
    chosen = expert_ids.reshape(rows * TOPK)
    onehot = (chosen[:, None] == jnp.arange(experts_here, dtype=jnp.int32)[None, :]).astype(
        jnp.int32
    )
    ranking = jnp.sum(onehot * (jnp.cumsum(onehot, axis=0) - 1), axis=1)
    slot_ids = chosen * capacity + ranking
    slot_table = jnp.arange(experts_here * capacity, dtype=jnp.int32)
    placing = jnp.any(slot_ids.reshape(rows, TOPK)[None, :, :] == slot_table[:, None, None], axis=2)
    dispatch = jnp.dot(
        placing.astype(jnp.bfloat16), normed, preferred_element_type=jnp.float32
    ).astype(jnp.bfloat16)
    dispatch = dispatch.reshape(experts_here, capacity, width)
    arrived = lax.all_to_all(dispatch, "ctx", split_axis=0, concat_axis=0, tiled=True)
    pooled = lax.all_gather(arrived, "head", axis=0, tiled=True).reshape(-1, width)
    produced = lax.psum_scatter(
        expert_half(pooled, w_gate[0], w_up[0], w_down_t[0]).astype(jnp.bfloat16),
        "head",
        scatter_dimension=0,
        tiled=True,
    )
    outgoing = produced.reshape(experts_here, capacity, width)
    returned = lax.all_to_all(outgoing, "ctx", split_axis=0, concat_axis=0, tiled=True)
    picked = returned.reshape(experts_here * capacity, width)[slot_ids].reshape(rows, TOPK, width)
    combine = route_scores / jnp.sum(route_scores, axis=1, keepdims=True)
    combined = jnp.sum(picked.astype(jnp.float32) * combine[:, :, None], axis=1)
    return (widened + routed_factor * combined).astype(jnp.bfloat16)


def solution(mesh):
    placed = (
        P("ctx", ("head", "ep"), None),
        P("ctx", None),
        P(("head", "ep"), None, None),
        P(("head", "ep"), None),
        P(("ctx", "head", "ep"), None),
        P(),
        P("ctx", None, "head"),
        P("ctx", None, "head"),
        P("ctx", None, "head"),
        P(("ctx", "head", "ep"), None),
        P(("ctx", "head", "ep"), None),
    )
    return jax.shard_map(
        per_device,
        mesh=mesh,
        in_specs=placed,
        out_specs=P(("ctx", "head", "ep"), None),
        check_vma=False,
    )
```

profile of v0, /device:TPU:2, one launch (start us, length us, event | category | flops | bytes accessed | tf_op | source)
XLA Modules:
  0.0 361.9 jit_solution(9355693872994284279)
XLA Ops:
  6.5 2.3 copy.44
  8.9 0.0 all-gather.6.cloned.1.call-start
  8.9 0.7 all-gather.6.cloned.1.call-update
  9.6 0.8 copy.47
  10.4 0.1 eq.35
  10.5 0.6 reduce-window.6
  11.1 0.2 slice_reduce_fusion
  11.3 0.1 bitcast_bitcast_fusion
  11.4 0.1 reduce_sum.51
  11.5 121.7 %all-gather.4.cloned.1.call-done = bf16[8192,576]{1,0:T(8,128)(2,1)} async-done(((bf16[512,576]{1,0:T(8,128)(2,1)}), bf16[8192,576]{1,0:T(8,128)(2,1)}) %all-gather.4.cloned.1.call-update) | async-done | bytes 9437200 | tf_op jit(solution)/shard_map/all_gather | solution.py:58
  133.3 33.9 %conditional.1 = (f32[512]{0:T(512)S(1)}, f32[512,512]{1,0:T(8,128)S(1)}) conditional(s32[]{:T(128)} %convert_element_type.56, (s32[]{:T(128)}, s32[512]{0:T(512)S(1)}, bf16[512,1,576]{0,2,1:T(8,128)(2,1)}, bf16[8192,576]{1,0:T(8,128)(2,1)}) %tuple.16, () %tuple.17), branch_computations={%region_0.3_spmd, %region_3.4_spmd} | conditional | flops 9193914368 | bytes 107567152 | solution.py:79
  133.3 16.1 %fusion = (f32[512]{0:T(512)S(1)}, f32[512,8192]{1,0:T(8,128)}) fusion(s32[512]{0:T(512)S(1)} %broadcast_add_fusion, bf16[8192,576]{1,0:T(8,128)(2,1)} %get-tuple-element.48, bf16[512,1,576]{0,2,1:T(8,128)(2,1)} %get-tuple-element.54), kind=kOutput, calls=%fused_computation.4 | convolution fusion | flops 4848614912 | bytes 26808320 | tf_op jit(solution)/shard_map/cond/branch_0_fun/dot_general | solution.py:64
  149.4 9.1 %fusion.3 = f32[512,512]{1,0:T(8,128)S(1)} fusion(bf16[8192,576]{1,0:T(8,128)(2,1)S(1)} %copy-done.4, f32[512,8192]{1,0:T(8,128)} %get-tuple-element.60, f32[512]{0:T(512)S(1)} %broadcast_maximum_fusion, s32[512]{0:T(512)S(1)} %broadcast_add_fusion), kind=kOutput, calls=%fused_computation.7 | convolution fusion | flops 4320133120 | bytes 26218496 | tf_op jit(solution)/shard_map/cond/branch_0_fun/dot_general | solution.py:76
  158.5 8.8 %fusion.2 = f32[512]{0:T(512)S(1)} fusion(f32[512,8192]{1,0:T(8,128)} %get-tuple-element.60, f32[512]{0:T(512)S(1)} %broadcast_maximum_fusion, s32[512]{0:T(512)S(1)} %broadcast_add_fusion), kind=kLoop, calls=%fused_computation.6 | loop fusion | flops 25165312 | bytes 16783360 | tf_op jit(solution)/shard_map/cond/branch_0_fun/reduce_sum | solution.py:74
  167.2 0.4 fusion.27
  167.6 0.5 broadcast.98
  168.1 0.7 reduce.2
  168.8 0.7 reshape.115
  169.5 6.2 %all-to-all-start = ((bf16[16,2,2048]{2,1,0:T(2,128)(2,1)}), bf16[16,2,2048]{2,1,0:T(2,128)(2,1)S(1)}, u32[]{:S(2)}, u32[]{:S(2)}) async-start(bf16[16,2,2048]{2,1,0:T(2,128)(2,1)} %reshape.115), calls=%async_computation | async-start | bytes 262144 | tf_op jit(solution)/shard_map/all_to_all | solution.py:90
  175.7 0.2 all-gather.8.cloned.1.call-start
  175.9 0.1 copy.51
  176.0 0.1 fusion.35
  176.1 9.2 %all-to-all-done = bf16[16,2,2048]{2,1,0:T(2,128)(2,1)S(1)} async-done(((bf16[16,2,2048]{2,1,0:T(2,128)(2,1)}), bf16[16,2,2048]{2,1,0:T(2,128)(2,1)S(1)}, u32[]{:S(2)}, u32[]{:S(2)}) %all-to-all-start) | async-done | bytes 131104 | tf_op jit(solution)/shard_map/all_to_all | solution.py:90
  185.3 0.1 reshape.116
  185.5 0.1 copy.46
  185.5 27.7 %all-gather.6.cloned.1.call-done = bf16[2048,2048]{1,0:T(8,128)(2,1)} async-done(((bf16[128,2048]{1,0:T(8,128)(2,1)}), bf16[2048,2048]{1,0:T(8,128)(2,1)}) %all-gather.6.cloned.1.call-update) | async-done | bytes 8388624 | tf_op jit(solution)/shard_map/all_gather | solution.py:93
  213.2 4.9 %fusion.20 = bf16[32,2048]{1,0:T(8,128)(2,1)S(1)} fusion(bf16[2048,2048]{1,0:T(8,128)(2,1)} %all-gather.6.cloned.1.call-done, bf16[32,2048]{1,0:T(8,128)(2,1)S(1)} %copy-done.1, bf16[4,8,16,128]{3,2,1,0:T(8,128)(2,1)S(1)} %bitcast.57), kind=kOutput, calls=%fused_computation.28 | convolution fusion | flops 268632064 | bytes 8781824 | tf_op jit(solution)/shard_map/dot_general | solution.py:26
  218.1 0.1 fusion.31
  218.3 1.5 convolution_convert_fusion.1
  219.8 2.5 reshape.100
  222.3 34.7 %all_to_all.25 = bf16[16,15,2048]{2,1,0:T(8,128)(2,1)S(1)} all-to-all(bf16[16,15,2048]{2,1,0:T(8,128)(2,1)} %reshape.100), channel_id=1, replica_groups=mesh['ctx'=16,'head'=2,'ep'=8] {'ctx'}, dimensions={0} | all-to-all | bytes 1966080 | tf_op jit(solution)/shard_map/all_to_all | solution.py:115
  257.0 1.5 copy.52
  258.6 11.4 %all-gather.8.cloned.1.call-done = bf16[32,15,2048]{2,0,1:T(8,128)(2,1)} async-done(((bf16[16,15,2048]{2,0,1:T(8,128)(2,1)}), bf16[32,15,2048]{2,0,1:T(8,128)(2,1)}) %all-gather.8.cloned.1.call-update) | async-done | bytes 1966096 | tf_op jit(solution)/shard_map/all_gather | solution.py:116
  270.0 4.0 %copy.53 = bf16[32,15,2048]{2,1,0:T(8,128)(2,1)} copy(bf16[32,15,2048]{2,0,1:T(8,128)(2,1)} %all-gather.8.cloned.1.call-done) | data formatting | bytes 3932160 | tf_op jit(solution)/shard_map/all_gather | solution.py:116
  274.0 2.8 reshape.101
  276.8 5.2 %fusion.18 = f32[480,704]{0,1:T(8,128)} fusion(bf16[480,2048]{1,0:T(8,128)(2,1)} %reshape.101, bf16[1,2048,704]{1,2,0:T(8,128)(2,1)} %param.19), kind=kOutput, calls=%fused_computation.24 | convolution fusion | flops 1384120320 | bytes 6201344 | tf_op jit(solution)/shard_map/dot_general | solution.py:17
  282.0 7.5 %convolution_convert_fusion = bf16[480,2048]{1,0:T(8,128)(2,1)} fusion(bf16[1,2048,704]{1,2,0:T(8,128)(2,1)S(1)} %copy-done, bf16[480,2048]{1,0:T(8,128)(2,1)} %reshape.101, bf16[1,2048,704]{1,2,0:T(8,128)(2,1)} %param.20, f32[480,704]{0,1:T(8,128)} %fusion.18), kind=kOutput, calls=%fused_computation.20 | convolution fusion | flops 2771251200 | bytes 11051008 | tf_op jit(solution)/shard_map/dot_general | solution.py:20
  289.5 16.3 %reduce-scatter.2.cloned.1.call-done = bf16[240,2048]{1,0:T(8,128)(2,1)} async-done(((bf16[480,2048]{1,0:T(8,128)(2,1)}), bf16[240,2048]{1,0:T(8,128)(2,1)}) %reduce-scatter.2.cloned.1.call-update) | async-done | bytes 983056 | tf_op jit(solution)/shard_map/reduce_scatter | solution.py:117
  305.8 2.5 reshape.102
  308.3 8.5 %all-to-all-start.2 = ((bf16[16,15,2048]{2,1,0:T(8,128)(2,1)}), bf16[16,15,2048]{2,1,0:T(8,128)(2,1)}, u32[]{:S(2)}, u32[]{:S(2)}) async-start(bf16[16,15,2048]{2,1,0:T(8,128)(2,1)} %reshape.102), calls=%async_computation.3 | async-start | bytes 2097152 | tf_op jit(solution)/shard_map/all_to_all | solution.py:124
  316.8 0.1 mul.79
  316.9 0.1 copy.54
  317.0 26.1 %all-to-all-done.2 = bf16[16,15,2048]{2,1,0:T(8,128)(2,1)} async-done(((bf16[16,15,2048]{2,1,0:T(8,128)(2,1)}), bf16[16,15,2048]{2,1,0:T(8,128)(2,1)}, u32[]{:S(2)}, u32[]{:S(2)}) %all-to-all-start.2) | async-done | bytes 983072 | tf_op jit(solution)/shard_map/all_to_all | solution.py:124
  343.1 2.5 reshape.103
  345.7 4.1 %gather_fusion = bf16[192,2048]{1,0:T(8,128)(2,1)} fusion(bf16[240,2048]{1,0:T(8,128)(2,1)} %reshape.103, s32[1024]{0:T(1024)S(1)} %pad_clamp_fusion), kind=kCustom, calls=%fused_computation | custom fusion | bytes 1573632 | tf_op jit(solution)/shard_map/gather | solution.py:125
  349.8 2.5 reshape.105
  352.3 2.3 multiply_reduce_fusion
  354.7 0.7 fusion.34
  (32 shorter events, 0.3 us)
Async XLA Ops:
  6.5 275.5 %copy-start = (bf16[1,2048,704]{1,2,0:T(8,128)(2,1)S(1)}, bf16[1,2048,704]{1,2,0:T(8,128)(2,1)}, u32[]{:S(2)}) copy-start(bf16[1,2048,704]{1,2,0:T(8,128)(2,1)} %param.21) | copy-start | bytes 8650756
  6.5 126.7 %all-gather.4.cloned.1.call-start = ((), (), s32[]{:S(2)}) async-start(), calls=%async_computation.4 | async-start | bytes 11141120 | tf_op jit(solution)/shard_map/all_gather | solution.py:58
  8.9 204.3 %all-gather.6.cloned.1.call-start = ((), (), s32[]{:S(2)}) async-start(), calls=%async_computation.5 | async-start | bytes 8912896 | tf_op jit(solution)/shard_map/all_gather | solution.py:93
  133.3 33.9 %copy-start.5 = (bf16[1,512,128]{2,1,0:T(8,128)(2,1)S(1)}, bf16[1,512,128]{2,1,0:T(8,128)(2,1)}, u32[]{:S(2)}) copy-start(bf16[1,512,128]{2,1,0:T(8,128)(2,1)} %param.15) | copy-start | bytes 393220
  133.3 79.9 %copy-start.1 = (bf16[32,2048]{1,0:T(8,128)(2,1)S(1)}, bf16[32,2048]{1,0:T(8,128)(2,1)}, u32[]{:S(2)}) copy-start(bf16[32,2048]{1,0:T(8,128)(2,1)} %param.17) | copy-start | bytes 393220
  133.3 16.1 %copy-start.4 = (bf16[8192,576]{1,0:T(8,128)(2,1)S(1)}, bf16[8192,576]{1,0:T(8,128)(2,1)}, u32[]{:S(2)}) copy-start(bf16[8192,576]{1,0:T(8,128)(2,1)} %get-tuple-element.48) | copy-start | bytes 28311556 | tf_op jit(solution)/shard_map/cond
  169.5 15.8 %all-to-all-start = ((bf16[16,2,2048]{2,1,0:T(2,128)(2,1)}), bf16[16,2,2048]{2,1,0:T(2,128)(2,1)S(1)}, u32[]{:S(2)}, u32[]{:S(2)}) async-start(bf16[16,2,2048]{2,1,0:T(2,128)(2,1)} %reshape.115), calls=%async_computation | async-start | bytes 262144 | tf_op jit(solution)/shard_map/all_to_all | solution.py:90
  175.7 94.3 %all-gather.8.cloned.1.call-start = ((), (), s32[]{:S(2)}) async-start(), calls=%async_computation.6 | async-start | bytes 2949120 | tf_op jit(solution)/shard_map/all_gather | solution.py:116
  185.5 32.8 %copy-start.3 = (f32[2048]{0:T(1024)S(1)}, f32[2048]{0:T(1024)}, u32[]{:S(2)}) copy-start(f32[2048]{0:T(1024)} %param.18) | copy-start | bytes 24580
  258.5 47.2 %reduce-scatter.2.cloned.1.call-start = ((), (), s32[]{:S(2)}) async-start(), calls=%async_computation.7 | async-start | bytes 2949120 | tf_op jit(solution)/shard_map/reduce_scatter | solution.py:117
  282.0 34.9 %copy-start.2 = (f32[32,6]{0,1:T(8,128)S(1)}, f32[32,6]{0,1:T(8,128)}, u32[]{:S(2)}) copy-start(f32[32,6]{0,1:T(8,128)} %param.23) | copy-start | bytes 2308
  308.3 34.8 %all-to-all-start.2 = ((bf16[16,15,2048]{2,1,0:T(8,128)(2,1)}), bf16[16,15,2048]{2,1,0:T(8,128)(2,1)}, u32[]{:S(2)}, u32[]{:S(2)}) async-start(bf16[16,15,2048]{2,1,0:T(8,128)(2,1)} %reshape.102), calls=%async_computation.3 | async-start | bytes 2097152 | tf_op jit(solution)/shard_map/all_to_all | solution.py:124
Sparse Core Ops, SparseCore 0:
  9.1 124.0 all-gather.3
  136.0 77.0 all-gather.5
  258.7 11.2 all-gather.7
  289.6 16.0 reduce-scatter.1
where the time goes:
time: 363 us; the launch traced here: 362 us
  waiting for transfers between devices  213 us (59%)
  matrix products  44.6 us (12%)
  blocking collectives  34.7 us (10%)
  local copies, waits for them, and re-layouts  27.7 us (8%)
  starting transfers between devices  15 us (4%)
  other arithmetic  13.5 us (4%)
  between operations  13.3 us (4%)
    all_gather x1, waiting for transfers between devices, per_device(): keys = lax.all_gather(kv_latent, 'ctx', axis=0, tiled=True)  122 us
    all_to_all x1, blocking collectives, per_device(): lax.all_to_all(dispatch, 'ctx', split_axis=0, concat_axis=0, tiled=True)  34.7 us
    all_gather x1, waiting for transfers between devices, per_device(): lax.all_gather(w_out, ('head', 'ep'), axis=0, tiled=True)  27.7 us
    all_to_all x1, waiting for transfers between devices, per_device(): lax.all_to_all(outgoing, 'ctx', split_axis=0, concat_axis=0, tiled=True)  26.1 us
    reduce_scatter x1, waiting for transfers between devices, per_device(): lax.psum_scatter(expert_half(pooled, w_gate[0], w_up[0], w_down_t[0]).ast...  16.3 us
    dot_general x1, matrix products, compute(): lax.dot_general(queries, keys, (((1,), (1,)), ((), ())), preferred_elemen...  16.1 us
    all_gather x1, waiting for transfers between devices, per_device(): lax.all_gather(arrived, 'head', axis=0, tiled=True).reshape(-1, width)  11.4 us
    all_to_all x1, waiting for transfers between devices, per_device(): lax.all_to_all(head_out, ('head', 'ep'), split_axis=0, concat_axis=1, til...  9.21 us
  transfers between devices with their start and end apart: 6, of which 6 were waited for; matrix products, arithmetic and copies ran while one was open for 11% of the time, Pallas kernels for 0%

commit v1 on v0

--- a/solution.py
+++ b/solution.py
@@ -1,16 +1,313 @@
 import jax
 import jax.numpy as jnp
 from jax import lax
+from jax.experimental import pallas as pl
+from jax.experimental.pallas import tpu as pltpu
 from jax.sharding import PartitionSpec as P
 
+MESH = pl.DeviceIdType.MESH
+BF16, F32 = jnp.bfloat16, jnp.float32
+NT = (((1,), (1,)), ((), ()))
+NN = (((1,), (0,)), ((), ()))
 ROPE = 64
 NOPE = 128
 TOPK = 6
-
-
+LOG2E = 1.4426950408889634
+EXP_SCALE = (NOPE + ROPE) ** (-0.5) * LOG2E
 routed_factor = 2.446
 norm_epsilon = 1e-06
 masked_score = -1e30
+
+
+def dot(a, b, dims=NN):
+    return lax.dot_general(a, b, dims, preferred_element_type=F32)
+
+
+def coords():
+    ctx, core, ep = lax.axis_index("ctx"), lax.axis_index("head"), lax.axis_index("ep")
+    x_lo, z, y, x_hi = ctx // 8, ctx % 8, ep // 2, ep % 2
+    return x_hi * 2 + x_lo, y, z, core
+
+
+def device(x, y, z, core):
+    x, y, z = (x + 4) % 4, (y + 4) % 4, (z + 8) % 8
+    return ((x % 2) * 8 + z, core, y * 2 + x // 2)
+
+
+def greet(partners):
+    barrier = pltpu.get_barrier_semaphore()
+    for partner in partners:
+        pl.semaphore_signal(barrier, inc=1, device_id=partner, device_id_type=MESH)
+    pl.semaphore_wait(barrier, len(partners))
+
+
+def remote(src, dst, send_sem, recv_sem, target):
+    return pltpu.make_async_remote_copy(
+        src_ref=src, dst_ref=dst, send_sem=send_sem, recv_sem=recv_sem,
+        device_id=target, device_id_type=MESH,
+    )
+
+
+SLOT = {0: 0, 1: 1, 7: 2, 2: 3, 6: 4, 3: 5, 5: 6, 4: 7}
+
+
+def attention_kernel(
+    q_ref, kv_ref, wv_ref, wo_ref, out_ref, wo4_ref,
+    keys, q_far, wv_far, high, denom, accum, back, back_lse, far_out, far_lse,
+    z_send, z_recv, y_send, y_recv, s_send, s_recv, q_send, q_recv, w_send, w_recv, own_sem,
+):
+    x, y, z, core = coords()
+    x_lo, x_hi, parity = x % 2, x // 2, y % 2
+    tokens, latent = q_ref.shape[0], wv_ref.shape[0]
+    half, quarter = tokens // 2, tokens // 4
+    z_up, z_down = device(x, y, z + 1, core), device(x, y, z - 1, core)
+    y_up, y_down = device(x, y + 1, z, core), device(x, y - 1, z, core)
+    x_up, x_down = device(x + 1, y, z, core), device(x - 1, y, z, core)
+    sibling = device(x, y, z, 1 - core)
+    y_to = device(x, y + 1 - 2 * core, z, core)
+    x_to = device(x - 1 + 2 * core, y, z, core)
+    x_from = device(x + 1 - 2 * core, y, z, core)
+    x_other = device(x - 1 + 2 * x_lo, y, z, core)
+
+    row_mine = parity * half + core * quarter
+    row_other = (1 - parity) * half + core * quarter
+    row_sib_mine = parity * half + (1 - core) * quarter
+    row_sib_other = (1 - parity) * half + (1 - core) * quarter
+
+    def rows(k, start, size):
+        return keys.at[pl.ds(pl.multiple_of(SLOT[k] * tokens + start, 16), size)]
+
+    def z_copy(way, step):
+        target = z_up if way == 0 else z_down
+        k_dst = step if way == 0 else 8 - step
+        k_src = step - 1 if way == 0 else (8 - (step - 1)) % 8
+        start, size = row_mine, quarter
+        if step == 4:
+            size = quarter // 2
+            start = row_mine + way * size
+        if k_src == 0:
+            src = kv_ref.at[pl.ds(pl.multiple_of(start, 16), size)]
+        else:
+            src = rows(k_src, start, size)
+        return remote(src, rows(k_dst, start, size), z_send.at[way, step - 1], z_recv.at[way, step - 1], target)
+
+    def y_copy(k, start):
+        return remote(rows(k, start, quarter), rows(k, start, quarter), y_send.at[k - 1], y_recv.at[k - 1], y_to)
+
+    def s_copy(k, which, start):
+        return remote(rows(k, start, quarter), rows(k, start, quarter), s_send.at[which, k - 1], s_recv.at[which, k - 1], sibling)
+
+    q_copy = remote(q_ref, q_far, q_send.at[0], q_recv.at[0], x_to)
+    wv_copy = remote(wv_ref, wv_far, q_send.at[1], q_recv.at[1], x_to)
+    back_copy = remote(back, far_out, q_send.at[2], q_recv.at[2], x_from)
+    lse_copy = remote(back_lse, far_lse, q_send.at[3], q_recv.at[3], x_from)
+    mine, partner = core * 2 + x_hi, core * 2 + 1 - x_hi
+    wo_own = pltpu.make_async_copy(wo_ref, wo4_ref.at[mine], own_sem)
+    wo_sib = remote(wo_ref, wo4_ref.at[mine], w_send.at[0], w_recv.at[0], sibling)
+    wo_far = remote(wo_ref, wo4_ref.at[mine], w_send.at[1], w_recv.at[1], x_other)
+    wo_fwd = remote(wo4_ref.at[partner], wo4_ref.at[partner], w_send.at[2], w_recv.at[2], sibling)
+
+    greet([z_up, z_down, y_up, y_down, x_up, x_down, sibling])
+
+    z_copy(0, 1).start()
+    z_copy(1, 1).start()
+
+    @pl.when(x_lo == 1)
+    def _():
+        q_copy.start()
+        wv_copy.start()
+
+    wo_own.start()
+    wo_sib.start()
+    wo_far.start()
+
+    keys[0:tokens] = kv_ref[...]
+    high[...] = jnp.full(high.shape, masked_score, F32)
+    denom[...] = jnp.zeros(denom.shape, F32)
+    accum[...] = jnp.zeros(accum.shape, F32)
+
+    def tile(which, queries, slot, count, change=None):
+        block = keys[slot * tokens:(slot + count) * tokens]
+        chunks = [slice(0, half), slice(half, tokens)]
+        scores = [dot(queries[rows_at], block, NT) for rows_at in chunks]
+        for rows_at, score in zip(chunks, scores):
+            if change is not None:
+                score = change(score, rows_at.start)
+            at = (which, rows_at, slice(None))
+            old = high[at]
+            new = jnp.maximum(old, jnp.max(score, axis=1, keepdims=True))
+            keep = jnp.exp2((old - new) * EXP_SCALE)
+            weight = jnp.exp2((score - new) * EXP_SCALE)
+            denom[at] = denom[at] * keep + jnp.sum(weight, axis=1, keepdims=True)
+            high[at] = new
+            accum[at] = accum[at] * keep + dot(weight.astype(BF16), block[:, :latent])
+
+    def diagonal(score, start):
+        row = start + lax.broadcasted_iota(jnp.int32, score.shape, 0)
+        column = lax.broadcasted_iota(jnp.int32, score.shape, 1)
+        return jnp.where(column <= row, score, masked_score)
+
+    def pair_mask(step):
+        def change(score, start):
+            column = lax.broadcasted_iota(jnp.int32, score.shape, 1)
+            first = jnp.where(z >= step, 0, tokens)
+            last = jnp.where(z + step >= 8, 2 * tokens, tokens)
+            return jnp.where((column >= first) & (column < last), score, masked_score)
+        return change
+
+    def own_pair(step):
+        both = (z >= step) & (z + step >= 8)
+        some = (z >= step) | (z + step >= 8)
+
+        @pl.when(both)
+        def _():
+            tile(0, q_ref, SLOT[step], 2)
+
+        @pl.when(some & jnp.logical_not(both))
+        def _():
+            tile(0, q_ref, SLOT[step], 2, pair_mask(step))
+
+    def far_tile(slot, count):
+        @pl.when(x_lo == 0)
+        def _():
+            tile(1, q_far, slot, count)
+
+    tile(0, q_ref, 0, 1, diagonal)
+
+    def after_z(step):
+        ks = [step, 8 - step] if step < 4 else [4]
+        z_copy(0, step).wait_recv()
+        z_copy(1, step).wait_recv()
+        if step < 4:
+            z_copy(0, step + 1).start()
+            z_copy(1, step + 1).start()
+        for k in ks:
+            y_copy(k, row_mine).start()
+            s_copy(k, 0, row_mine).start()
+
+    def after_y(step):
+        for k in ([step, 8 - step] if step < 4 else [4]):
+            y_copy(k, row_other).wait_recv()
+            s_copy(k, 1, row_other).start()
+
+    def after_s(step):
+        for k in ([step, 8 - step] if step < 4 else [4]):
+            s_copy(k, 0, row_sib_mine).wait_recv()
+            s_copy(k, 1, row_sib_other).wait_recv()
+
+    after_z(1)
+    after_y(1)
+
+    @pl.when(x_lo == 0)
+    def _():
+        q_copy.wait_recv()
+        wv_copy.wait_recv()
+
+    far_tile(0, 1)
+    after_z(2)
+    after_s(1)
+    own_pair(1)
+    after_y(2)
+    far_tile(1, 2)
+    after_z(3)
+    after_s(2)
+    own_pair(2)
+    after_y(3)
+    far_tile(3, 2)
+    after_z(4)
+    after_s(3)
+    own_pair(3)
+    after_y(4)
+    far_tile(5, 2)
+    wo_far.wait_recv()
+    wo_fwd.start()
+    after_s(4)
+    far_tile(7, 1)
+
+    @pl.when(x_lo == 0)
+    def _():
+        latent_far = (accum[1] / denom[1]).astype(BF16)
+        back[...] = dot(latent_far, wv_far[...]).astype(BF16)
+        lse = high[1] * EXP_SCALE + jnp.log2(denom[1])
+        back_lse[...] = jnp.broadcast_to(lse, (tokens, 128)).T[0:8]
+        back_copy.start()
+        lse_copy.start()
+
+    @pl.when(z >= 4)
+    def _():
+        tile(0, q_ref, 7, 1)
+
+    head_out = dot((accum[0] / denom[0]).astype(BF16), wv_ref[...])
+
+    @pl.when(x_lo == 0)
+    def _():
+        out_ref[...] = head_out.astype(BF16)
+
+    @pl.when(x_lo == 1)
+    def _():
+        lse = high[0] * EXP_SCALE + jnp.log2(denom[0])
+        back_copy.wait_recv()
+        lse_copy.wait_recv()
+        other = jnp.broadcast_to(far_lse[0:1], (128, tokens)).T
+        top = jnp.maximum(lse, other)
+        near_part, far_part = jnp.exp2(lse - top), jnp.exp2(other - top)
+        out_ref[...] = ((head_out * near_part + far_out[...].astype(F32) * far_part) / (near_part + far_part)).astype(BF16)
+
+    wo_sib.wait_recv()
+    wo_fwd.wait_recv()
+    wo_own.wait()
+    for copy in (wo_sib, wo_far, wo_fwd):
+        copy.wait_send()
+    for step in range(1, 5):
+        z_copy(0, step).wait_send()
+        z_copy(1, step).wait_send()
+    for k in range(1, 8):
+        y_copy(k, row_mine).wait_send()
+        s_copy(k, 0, row_mine).wait_send()
+        s_copy(k, 1, row_other).wait_send()
+
+    @pl.when(x_lo == 1)
+    def _():
+        q_copy.wait_send()
+        wv_copy.wait_send()
+
+    @pl.when(x_lo == 0)
+    def _():
+        back_copy.wait_send()
+        lse_copy.wait_send()
+
+
+def attend(queries, kv, w_value, w_out):
+    tokens, width = queries.shape
+    latent, values = w_value.shape
+    dma = pltpu.SemaphoreType.DMA
+    vmem = pl.BlockSpec(memory_space=pltpu.VMEM)
+    hbm = pl.BlockSpec(memory_space=pl.ANY)
+    return pl.pallas_call(
+        attention_kernel,
+        out_shape=(
+            jax.ShapeDtypeStruct((tokens, values), BF16),
+            jax.ShapeDtypeStruct((4,) + w_out.shape, BF16),
+        ),
+        in_specs=[vmem, vmem, vmem, hbm],
+        out_specs=(vmem, hbm),
+        scratch_shapes=[
+            pltpu.VMEM((8 * tokens, width), BF16),
+            pltpu.VMEM((tokens, width), BF16),
+            pltpu.VMEM((latent, values), BF16),
+            pltpu.VMEM((2, tokens, 1), F32),
+            pltpu.VMEM((2, tokens, 1), F32),
+            pltpu.VMEM((2, tokens, latent), F32),
+            pltpu.VMEM((tokens, values), BF16),
+            pltpu.VMEM((8, tokens), F32),
+            pltpu.VMEM((tokens, values), BF16),
+            pltpu.VMEM((8, tokens), F32),
+            dma((2, 4)), dma((2, 4)), dma((7,)), dma((7,)), dma((2, 7)), dma((2, 7)),
+            dma((4,)), dma((4,)), dma((3,)), dma((3,)), dma,
+        ],
+        name="attention",
+        compiler_params=pltpu.CompilerParams(collective_id=0, has_side_effects=True, vmem_limit_bytes=56 << 20),
+    )(queries, kv, w_value, w_out)
 
 
 def expert_half(inputs, gate_part, up_part, down_part):
@@ -44,49 +341,8 @@
     latent_width = w_value.shape[1]
     width = resid.shape[1]
     rows = resid.shape[0]
-    query_rows = tokens_here * heads_here
-    score_scale = (NOPE + ROPE) ** (-0.5)
-    queries = q_latent.reshape(query_rows, q_latent.shape[2])
-    first_token = lax.axis_index("ctx") * tokens_here
-    last_token = first_token + tokens_here - 1
-    query_pos = first_token + jnp.arange(query_rows, dtype=jnp.int32) // heads_here
-    start_state = (
-        jnp.full((query_rows,), masked_score, jnp.float32),
-        jnp.zeros((query_rows,), jnp.float32),
-        jnp.zeros((query_rows, latent_width), jnp.float32),
-    )
-    keys = lax.all_gather(kv_latent, "ctx", axis=0, tiled=True)
-    count = keys.shape[0]
-
-    def compute(state):
-        highest, denominator, accum = state
-        scores = (
-            lax.dot_general(
-                queries, keys, (((1,), (1,)), ((), ())), preferred_element_type=jnp.float32
-            )
-            * score_scale
-        )
-        key_pos = jnp.arange(count, dtype=jnp.int32)
-        visible = key_pos[None, :] <= query_pos[:, None]
-        scores = jnp.where(visible, scores, masked_score)
-        new_highest = jnp.maximum(highest, jnp.max(scores, axis=1))
-        weights = jnp.where(visible, jnp.exp(scores - new_highest[:, None]), 0.0)
-        denominator = jnp.sum(weights, axis=1)
-        values = keys[:, :latent_width]
-        accum = jnp.dot(weights.astype(jnp.bfloat16), values, preferred_element_type=jnp.float32)
-        return (new_highest, denominator, accum)
-
-    highest, denominator, accum = lax.cond(
-        jnp.int32(0) > last_token, lambda state: state, compute, start_state
-    )
-    latent_out = (
-        (accum / denominator[:, None])
-        .astype(jnp.bfloat16)
-        .reshape(tokens_here, heads_here, latent_width)
-    )
-    head_out = jnp.einsum(
-        "thl,hlv->thv", latent_out, w_value, preferred_element_type=jnp.float32
-    ).astype(jnp.bfloat16)
+    head_out, _ = attend(q_latent.reshape(tokens_here, q_latent.shape[2]), kv_latent, w_value[0], w_out)
+    head_out = head_out.reshape(tokens_here, 1, w_value.shape[2])
     grouped = lax.all_to_all(head_out, ("head", "ep"), split_axis=0, concat_axis=1, tiled=True)
     flat_heads = grouped.reshape(rows, grouped.shape[1] * grouped.shape[2])
     attended = make_projection(

time: 363 us -> 248 us (0.68)
  waiting for transfers between devices: 213 us -> 61.7 us
  Pallas kernels: 0 us -> 64.6 us
  matrix products: 44.6 us -> 19.1 us
  other arithmetic: 13.5 us -> 5.66 us
  starting transfers between devices: 15 us -> 20.7 us
    all_gather x1 -> x0, waiting for transfers between devices: 122 us -> none  [per_device(): keys = lax.all_gather(kv_latent, 'ctx', axis=0, tiled=True)]
    pallas_call x0 -> x1, Pallas kernels: none -> 64.6 us  [attend(): pl.pallas_call(attention_kernel, out_shape=(jax.ShapeDtypeStruct((tokens,...]
    all_gather x1, waiting for transfers between devices: 27.7 us -> 0.02 us  [per_device(): lax.all_gather(w_out, ('head', 'ep'), axis=0, tiled=True)]
    dot_general x3 -> x0, matrix products: 25.5 us -> none  [the longest x1 16.1 us: compute(): lax.dot_general(queries, keys, (((1,), (1,)), ((), ())), preferred_elemen...]
    reduce_sum x1 -> x0, other arithmetic: 8.76 us -> none  [compute(): denominator = jnp.sum(weights, axis=1)]
    all_to_all x1, starting transfers between devices: 6.17 us -> 11.9 us  [per_device(): lax.all_to_all(head_out, ('head', 'ep'), split_axis=0, concat_axis=1, til...]
  transfers between devices with their start and end apart: 6 -> 5, of which waited for: 6 -> 4; matrix products, arithmetic and copies ran while one was open for 11% -> 3% of each run, Pallas kernels for 0% -> 26%
where the time goes in v1:
time: 248 us; the launch traced here: 247 us
  Pallas kernels  64.6 us (26%)
  waiting for transfers between devices  61.7 us (25%)
  blocking collectives  33.6 us (14%)
  local copies, waits for them, and re-layouts  28 us (11%)
  starting transfers between devices  20.7 us (8%)
  matrix products  19.1 us (8%)
  between operations  13.3 us (5%)
  other arithmetic  5.66 us (2%)
    pallas_call x1, Pallas kernels, attend(): pl.pallas_call(attention_kernel, out_shape=(jax.ShapeDtypeStruct((tokens,...  64.6 us
    all_to_all x1, blocking collectives, per_device(): lax.all_to_all(dispatch, 'ctx', split_axis=0, concat_axis=0, tiled=True)  33.6 us
    all_to_all x1, waiting for transfers between devices, per_device(): lax.all_to_all(outgoing, 'ctx', split_axis=0, concat_axis=0, tiled=True)  26.1 us
    reduce_scatter x1, waiting for transfers between devices, per_device(): lax.psum_scatter(expert_half(pooled, w_gate[0], w_up[0], w_down_t[0]).ast...  16.2 us
    all_to_all x1, starting transfers between devices, per_device(): lax.all_to_all(head_out, ('head', 'ep'), split_axis=0, concat_axis=1, til...  11.9 us
    all_gather x1, waiting for transfers between devices, per_device(): lax.all_gather(arrived, 'head', axis=0, tiled=True).reshape(-1, width)  11.8 us
    all_to_all x1, starting transfers between devices, per_device(): lax.all_to_all(outgoing, 'ctx', split_axis=0, concat_axis=0, tiled=True)  8.49 us
    dot_general x1, matrix products, expert_half(): lax.dot_general(hidden, down_part, (((1,), (1,)), ((), ())), preferred_el...  7.46 us
  transfers between devices with their start and end apart: 5, of which 4 were waited for; matrix products, arithmetic and copies ran while one was open for 3% of the time, Pallas kernels for 26%

profile of v1, /device:TPU:2, one launch (start us, length us, event | category | flops | bytes accessed | tf_op | source)
XLA Modules:
  0.0 246.7 jit_solution(2541689890714215896)
XLA Ops:
  6.5 0.7 all-gather.3.cloned.1.call-update
  7.3 2.2 copy.46
  9.5 1.1 copy.47.kv_ref
  10.6 64.6 %attention.1 = (bf16[512,128]{1,0:T(8,128)(2,1)}, bf16[4,128,2048]{2,1,0:T(8,128)(2,1)}) custom-call(bf16[512,576]{1,0:T(8,128)(2,1)} %bitcast.45, bf16[512,576]{1,0:T(8,128)(2,1)} %copy.47.kv_ref, bf16[512,128]{1,0:T(8,128)(2,1)} %bitcast.49, bf16[128,2048]{1,0:T(8,128)(2,1)} %wo_ref.1), custom_call_target="tpu_custom_call" | custom-call | tf_op jit(solution)/shard_map/attention/pallas_call | solution.py:286
  75.2 0.5 broadcast.68
  75.7 1.6 reduce.2
  77.3 0.7 reshape.103
  78.0 11.9 %all-to-all-start = ((bf16[16,2,2048]{2,1,0:T(2,128)(2,1)}), bf16[16,2,2048]{2,1,0:T(2,128)(2,1)S(1)}, u32[]{:S(2)}, u32[]{:S(2)}) async-start(bf16[16,2,2048]{2,1,0:T(2,128)(2,1)} %reshape.103), calls=%async_computation | async-start | bytes 262144 | tf_op jit(solution)/shard_map/all_to_all | solution.py:346
  89.9 0.0 all-gather.5.cloned.1.call-start
  90.0 0.1 copy.50
  90.1 0.1 eq.35
  90.2 0.6 reduce-window.6
  90.8 0.2 slice_reduce_fusion
  91.0 0.1 bitcast_bitcast_fusion
  91.1 0.1 reduce_sum.41
  91.2 0.1 copy.54
  91.3 0.1 fusion.19
  91.4 6.8 %all-to-all-done = bf16[16,2,2048]{2,1,0:T(2,128)(2,1)S(1)} async-done(((bf16[16,2,2048]{2,1,0:T(2,128)(2,1)}), bf16[16,2,2048]{2,1,0:T(2,128)(2,1)S(1)}, u32[]{:S(2)}, u32[]{:S(2)}) %all-to-all-start) | async-done | bytes 131104 | tf_op jit(solution)/shard_map/all_to_all | solution.py:346
  98.2 0.1 reshape.104
  98.3 0.1 copy.49
  98.4 0.0 all-gather.3.cloned.1.call-done
  98.4 0.0 copy-start.4
  98.5 4.9 %fusion.5 = bf16[32,2048]{1,0:T(8,128)(2,1)S(1)} fusion(bf16[2048,2048]{1,0:T(8,128)(2,1)} %all-gather.3.cloned.1.call-done, bf16[32,2048]{1,0:T(8,128)(2,1)S(1)} %copy-done.2, bf16[4,8,16,128]{3,2,1,0:T(8,128)(2,1)S(1)} %bitcast.46), kind=kOutput, calls=%fused_computation.9 | convolution fusion | flops 268632064 | bytes 8781824 | tf_op jit(solution)/shard_map/dot_general | solution.py:323
  103.4 0.1 fusion.15
  103.5 1.5 convolution_convert_fusion.1
  105.0 2.5 %reshape.88 = bf16[16,15,2048]{2,1,0:T(8,128)(2,1)} reshape(bf16[240,2048]{1,0:T(8,128)(2,1)} %convolution_convert_fusion.1) | data formatting | bytes 1966080 | tf_op jit(solution)/shard_map/reshape | solution.py:370
  107.5 33.6 %all_to_all.25 = bf16[16,15,2048]{2,1,0:T(8,128)(2,1)S(1)} all-to-all(bf16[16,15,2048]{2,1,0:T(8,128)(2,1)} %reshape.88), channel_id=1, replica_groups=mesh['ctx'=16,'head'=2,'ep'=8] {'ctx'}, dimensions={0} | all-to-all | bytes 1966080 | tf_op jit(solution)/shard_map/all_to_all | solution.py:371
  141.2 1.5 copy.55
  142.7 0.0 all-gather.5.cloned.1.call-update
  142.7 0.3 reduce-scatter.2.cloned.1.call-start
  143.0 11.8 %all-gather.5.cloned.1.call-done = bf16[32,15,2048]{2,0,1:T(8,128)(2,1)} async-done(((bf16[16,15,2048]{2,0,1:T(8,128)(2,1)}), bf16[32,15,2048]{2,0,1:T(8,128)(2,1)}) %all-gather.5.cloned.1.call-update) | async-done | bytes 1966096 | tf_op jit(solution)/shard_map/all_gather | solution.py:372
  154.8 4.0 %copy.56 = bf16[32,15,2048]{2,1,0:T(8,128)(2,1)} copy(bf16[32,15,2048]{2,0,1:T(8,128)(2,1)} %all-gather.5.cloned.1.call-done) | data formatting | bytes 3932160 | tf_op jit(solution)/shard_map/all_gather | solution.py:372
  158.8 2.8 %reshape.89 = bf16[480,2048]{1,0:T(8,128)(2,1)} reshape(bf16[32,15,2048]{2,1,0:T(8,128)(2,1)} %copy.56) | data formatting | bytes 3932160 | tf_op jit(solution)/shard_map/reshape | solution.py:372
  161.6 5.2 %fusion.3 = f32[480,704]{0,1:T(8,128)} fusion(bf16[480,2048]{1,0:T(8,128)(2,1)} %reshape.89, bf16[1,2048,704]{1,2,0:T(8,128)(2,1)} %param.17), kind=kOutput, calls=%fused_computation.5 | convolution fusion | flops 1384120320 | bytes 6201344 | tf_op jit(solution)/shard_map/dot_general | solution.py:314
  166.8 7.5 %convolution_convert_fusion = bf16[480,2048]{1,0:T(8,128)(2,1)} fusion(bf16[1,2048,704]{1,2,0:T(8,128)(2,1)S(1)} %copy-done, bf16[480,2048]{1,0:T(8,128)(2,1)} %reshape.89, bf16[1,2048,704]{1,2,0:T(8,128)(2,1)} %param.18, f32[480,704]{0,1:T(8,128)} %fusion.3), kind=kOutput, calls=%fused_computation.1 | convolution fusion | flops 2771251200 | bytes 11051008 | tf_op jit(solution)/shard_map/dot_general | solution.py:317
  174.2 0.0 reduce-scatter.2.cloned.1.call-update
  174.3 0.0 copy-start.3
  174.3 16.2 %reduce-scatter.2.cloned.1.call-done = bf16[240,2048]{1,0:T(8,128)(2,1)} async-done(((bf16[480,2048]{1,0:T(8,128)(2,1)}), bf16[240,2048]{1,0:T(8,128)(2,1)}) %reduce-scatter.2.cloned.1.call-update) | async-done | bytes 983056 | tf_op jit(solution)/shard_map/reduce_scatter | solution.py:373
  190.5 2.5 %reshape.90 = bf16[16,15,2048]{2,1,0:T(8,128)(2,1)} reshape(bf16[240,2048]{1,0:T(8,128)(2,1)} %reduce-scatter.2.cloned.1.call-done) | data formatting | bytes 1966080 | tf_op jit(solution)/shard_map/reshape | solution.py:379
  193.1 8.5 %all-to-all-start.2 = ((bf16[16,15,2048]{2,1,0:T(8,128)(2,1)}), bf16[16,15,2048]{2,1,0:T(8,128)(2,1)}, u32[]{:S(2)}, u32[]{:S(2)}) async-start(bf16[16,15,2048]{2,1,0:T(8,128)(2,1)} %reshape.90), calls=%async_computation.3 | async-start | bytes 2097152 | tf_op jit(solution)/shard_map/all_to_all | solution.py:380
  201.6 0.1 mul.71
  201.7 0.1 copy.57
  201.8 26.1 %all-to-all-done.2 = bf16[16,15,2048]{2,1,0:T(8,128)(2,1)} async-done(((bf16[16,15,2048]{2,1,0:T(8,128)(2,1)}), bf16[16,15,2048]{2,1,0:T(8,128)(2,1)}, u32[]{:S(2)}, u32[]{:S(2)}) %all-to-all-start.2) | async-done | bytes 983072 | tf_op jit(solution)/shard_map/all_to_all | solution.py:380
  227.9 2.5 %reshape.91 = bf16[240,2048]{1,0:T(8,128)(2,1)} reshape(bf16[16,15,2048]{2,1,0:T(8,128)(2,1)} %all-to-all-done.2) | data formatting | bytes 1966080 | tf_op jit(solution)/shard_map/reshape | solution.py:381
  230.4 4.1 %gather_fusion = bf16[192,2048]{1,0:T(8,128)(2,1)} fusion(bf16[240,2048]{1,0:T(8,128)(2,1)} %reshape.91, s32[1024]{0:T(1024)S(1)} %pad_clamp_fusion), kind=kCustom, calls=%fused_computation | custom fusion | bytes 1573632 | tf_op jit(solution)/shard_map/gather | solution.py:381
  234.6 2.5 %reshape.93 = f32[32,6,2048]{2,1,0:T(8,128)} reshape(bf16[192,2048]{1,0:T(8,128)(2,1)} %gather_fusion) | data formatting | bytes 2359296 | tf_op jit(solution)/shard_map/convert_element_type | solution.py:383
  237.1 2.3 multiply_reduce_fusion
  239.4 0.7 fusion.18
  (23 shorter events, 0.2 us)
Async XLA Ops:
  6.5 160.2 %copy-start = (bf16[1,2048,704]{1,2,0:T(8,128)(2,1)S(1)}, bf16[1,2048,704]{1,2,0:T(8,128)(2,1)}, u32[]{:S(2)}) copy-start(bf16[1,2048,704]{1,2,0:T(8,128)(2,1)} %param.19) | copy-start | bytes 8650756
  6.5 2.9 %copy-start.1 = (bf16[512,576]{0,1:T(8,128)(2,1)S(1)}, bf16[512,576]{0,1:T(8,128)(2,1)}, u32[]{:S(2)}) copy-start(bf16[512,576]{0,1:T(8,128)(2,1)} %param.12) | copy-start | bytes 1769476
  6.5 91.9 %all-gather.3.cloned.1.call-start = ((), (), s32[]{:S(2)}) async-start(), calls=%async_computation.4 | async-start | bytes 8912896 | tf_op jit(solution)/shard_map/all_gather | solution.py:349
  9.5 80.5 %copy-start.5 = (s32[32,6]{0,1:T(8,128)S(1)}, s32[32,6]{0,1:T(8,128)}, u32[]{:S(2)}) copy-start(s32[32,6]{0,1:T(8,128)} %param.20) | copy-start | bytes 2308
  10.6 87.9 %copy-start.2 = (bf16[32,2048]{1,0:T(8,128)(2,1)S(1)}, bf16[32,2048]{1,0:T(8,128)(2,1)}, u32[]{:S(2)}) copy-start(bf16[32,2048]{1,0:T(8,128)(2,1)} %param.15) | copy-start | bytes 393220
  78.0 20.2 %all-to-all-start = ((bf16[16,2,2048]{2,1,0:T(2,128)(2,1)}), bf16[16,2,2048]{2,1,0:T(2,128)(2,1)S(1)}, u32[]{:S(2)}, u32[]{:S(2)}) async-start(bf16[16,2,2048]{2,1,0:T(2,128)(2,1)} %reshape.103), calls=%async_computation | async-start | bytes 262144 | tf_op jit(solution)/shard_map/all_to_all | solution.py:346
  89.9 64.9 %all-gather.5.cloned.1.call-start = ((), (), s32[]{:S(2)}) async-start(), calls=%async_computation.5 | async-start | bytes 2949120 | tf_op jit(solution)/shard_map/all_gather | solution.py:372
  98.4 5.1 %copy-start.4 = (f32[2048]{0:T(1024)S(1)}, f32[2048]{0:T(1024)}, u32[]{:S(2)}) copy-start(f32[2048]{0:T(1024)} %param.16) | copy-start | bytes 24580
  142.7 47.8 %reduce-scatter.2.cloned.1.call-start = ((), (), s32[]{:S(2)}) async-start(), calls=%async_computation.6 | async-start | bytes 2949120 | tf_op jit(solution)/shard_map/reduce_scatter | solution.py:373
  174.3 27.4 %copy-start.3 = (f32[32,6]{0,1:T(8,128)S(1)}, f32[32,6]{0,1:T(8,128)}, u32[]{:S(2)}) copy-start(f32[32,6]{0,1:T(8,128)} %param.21) | copy-start | bytes 2308
  193.1 34.8 %all-to-all-start.2 = ((bf16[16,15,2048]{2,1,0:T(8,128)(2,1)}), bf16[16,15,2048]{2,1,0:T(8,128)(2,1)}, u32[]{:S(2)}, u32[]{:S(2)}) async-start(bf16[16,15,2048]{2,1,0:T(8,128)(2,1)} %reshape.90), calls=%async_computation.3 | async-start | bytes 2097152 | tf_op jit(solution)/shard_map/all_to_all | solution.py:380
Sparse Core Ops, SparseCore 0:
  10.1 80.6 all-gather.2
  142.8 11.9 all-gather.4
  174.4 16.0 reduce-scatter.1

commit v2 on v1

--- a/solution.py
+++ b/solution.py
@@ -310,17 +310,272 @@
     )(queries, kv, w_value, w_out)
 
 
-def expert_half(inputs, gate_part, up_part, down_part):
-    gate = jnp.dot(inputs, gate_part, preferred_element_type=jnp.float32)
-    upward = jnp.dot(inputs, up_part, preferred_element_type=jnp.float32)
-    hidden = (jax.nn.silu(gate) * upward).astype(jnp.bfloat16)
-    return lax.dot_general(
-        hidden, down_part, (((1,), (1,)), ((), ())), preferred_element_type=jnp.float32
-    )
-
-
-def make_projection(source, piece):
-    return jnp.dot(source, piece, preferred_element_type=jnp.float32)
+def layer_kernel(
+    heads_ref, wo_ref, resid_ref, gain_ref, share_ref, gate_ref, up_ref, down_ref, out_ref,
+    wo, gate, up, down, pool, proj, proj_out, y_in, after, rows_in, part, sib_in, x_out, x_in,
+    z_out, z_in,
+    load_sem, h_send, h_recv, y_send, y_recv, az_send, az_recv, ax_send, ax_recv, as_send, as_recv,
+    bs_send, bs_recv, bx_send, bx_recv, bz_send, bz_recv,
+):
+    x, y, z, core = coords()
+    x_lo, x_hi = x % 2, x // 2
+    count, width = resid_ref.shape
+    piece = count // 2
+    sibling = device(x, y, z, 1 - core)
+    z_way = (device(x, y, z + 1, core), device(x, y, z - 1, core))
+    x_to = device(x - 1 + 2 * core, y, z, core)
+    x_from = device(x + 1 - 2 * core, y, z, core)
+    across = device(x + 2, y, z, core)
+    across_sib = device(x + 2, y, z, 1 - core)
+    y_at = [device(x, y + d, z, core) for d in (1, 2, 3)]
+
+    loads = [
+        pltpu.make_async_copy(src, dst, load_sem.at[i])
+        for i, (src, dst) in enumerate(((wo_ref, wo), (gate_ref, gate), (up_ref, up), (down_ref, down)))
+    ]
+    for load in loads:
+        load.start()
+
+    mine = core * 2 + x_hi
+    head_copies = [
+        remote(heads_ref.at[c_to, :, x_to_hi], pool.at[mine], h_send.at[i], h_recv.at[i], target)
+        for i, (c_to, x_to_hi, target) in enumerate((
+            (1 - core, x_hi, sibling), (core, 1 - x_hi, across), (1 - core, 1 - x_hi, across_sib)))
+    ]
+    greet([sibling, x_to, x_from, across, across_sib] + y_at + list(z_way))
+    for copy in head_copies:
+        copy.start()
+    pool[mine] = heads_ref[core, :, x_hi]
+    loads[0].wait()
+    for copy in head_copies:
+        copy.wait_recv()
+    features = jnp.concatenate([pool[i].reshape(4 * count, pool.shape[3]) for i in range(4)], axis=1)
+    attended = dot(features, wo[...].reshape(features.shape[1], width)).reshape(4, count, width)
+    proj[...] = attended
+    proj_out[...] = attended.astype(BF16)
+    y_copies = [
+        remote(proj_out.at[(y + d) % 4], y_in.at[d - 1], y_send.at[d - 1], y_recv.at[d - 1], y_at[d - 1])
+        for d in (1, 2, 3)
+    ]
+    for copy in y_copies:
+        copy.start()
+    total = resid_ref[...].astype(F32) + proj[y]
+    for d, copy in enumerate(y_copies):
+        copy.wait_recv()
+        total = total + y_in[d].astype(F32)
+    after[...] = total.astype(BF16)
+    widened = after[...].astype(F32)
+    mean_square = jnp.mean(widened * widened, axis=1, keepdims=True)
+    normed = (widened * lax.rsqrt(mean_square + norm_epsilon) * gain_ref[...]).astype(BF16)
+    rows_in[0, core, 0, :, 0:width] = normed
+    rows_in[0, core, 0, :, width:] = share_ref[...]
+
+    def gather_z(way, step, chunk):
+        k_dst = step if way == 0 else 8 - step
+        k_src = step - 1 if way == 0 else (9 - step) % 8
+        at = pl.ds(chunk * piece, piece)
+        return remote(
+            rows_in.at[SLOT[k_src], core, 0, at], rows_in.at[SLOT[k_dst], core, 0, at],
+            az_send.at[way, step - 1, chunk], az_recv.at[way, step - 1, chunk], z_way[way])
+
+    def gather_x(k):
+        return remote(rows_in.at[SLOT[k], core, 0], rows_in.at[SLOT[k], core, 1], ax_send.at[k], ax_recv.at[k], x_to)
+
+    def gather_s(k, column, who):
+        at = rows_in.at[SLOT[k], who, column]
+        return remote(at, at, as_send.at[column, k], as_recv.at[column, k], sibling)
+
+    def return_s(slot, who):
+        return remote(part.at[slot, who], sib_in.at[slot], bs_send.at[slot], bs_recv.at[slot], sibling)
+
+    def return_x(slot):
+        return remote(x_out.at[slot], x_in.at[slot], bx_send.at[slot], bx_recv.at[slot], x_from)
+
+    def return_z(way, k, chunk):
+        k_dst = k - 1 if way == 1 else (k + 1) % 8
+        index = k_dst if way == 1 else (8 - k_dst) % 8
+        return remote(
+            z_out.at[way, index, chunk], z_in.at[way, index, chunk],
+            bz_send.at[way, index, chunk], bz_recv.at[way, index, chunk], z_way[way])
+
+    members = [[0], [1, 7], [2, 6], [3, 5], [4]]
+    slots = [[SLOT[k] for k in ks] for ks in members]
+
+    def experts(step):
+        first, number = slots[step][0], len(slots[step])
+        block = rows_in[first:first + number].reshape(number * 4 * count, rows_in.shape[4])
+        source, shares = block[:, :width], block[:, width:].astype(F32)
+        lane = lax.broadcasted_iota(jnp.int32, shares.shape, 1)
+        expert = lax.axis_index("ctx")
+        share = jnp.sum(jnp.where((lane == expert) | (lane == expert + 16), shares, 0.0), axis=1, keepdims=True)
+        gated = dot(source, gate[...])
+        hidden = (gated / (1.0 + jnp.exp(-gated)) * dot(source, up[...]) * share).astype(BF16)
+        made = dot(hidden, down[...], NT).astype(BF16)
+        part[first:first + number] = made.reshape(number, 2, 2, count, width)
+
+    def send_parts(step):
+        for slot in slots[step]:
+            return_s(slot, 1 - core).start()
+
+    def fold_siblings(step):
+        for slot in slots[step]:
+            return_s(slot, 1 - core).wait_recv()
+            x_out[slot] = (part[slot, core, 1].astype(F32) + sib_in[slot, 1].astype(F32)).astype(BF16)
+            return_x(slot).start()
+
+    def after_z(step):
+        for chunk in (0, 1):
+            for way in (0, 1):
+                if step == 4 and chunk != way:
+                    continue
+                gather_z(way, step, chunk).wait_recv()
+                if step < 3 or (step == 3 and chunk == way):
+                    gather_z(way, step + 1, chunk).start()
+        for k in members[step]:
+            gather_x(k).start()
+            gather_s(k, 0, core).start()
+
+    def after_x(step):
+        for k in members[step]:
+            gather_x(k).wait_recv()
+            gather_s(k, 1, core).start()
+
+    def after_s(step):
+        for k in members[step]:
+            gather_s(k, 0, 1 - core).wait_recv()
+            gather_s(k, 1, 1 - core).wait_recv()
+
+    for chunk in (0, 1):
+        for way in (0, 1):
+            gather_z(way, 1, chunk).start()
+    gather_x(0).start()
+    gather_s(0, 0, core).start()
+    for load in loads[1:]:
+        load.wait()
+    after_x(0)
+    after_s(0)
+    experts(0)
+    send_parts(0)
+    for step in (1, 2, 3, 4):
+        after_z(step)
+        if step > 1:
+            after_x(step - 1)
+            after_s(step - 1)
+            experts(step - 1)
+            send_parts(step - 1)
+            fold_siblings(step - 2)
+    after_x(4)
+    after_s(4)
+    experts(4)
+    send_parts(4)
+    fold_siblings(3)
+    fold_siblings(4)
+
+    def local_sum(k, chunk):
+        slot, at = SLOT[k], slice(chunk * piece, (chunk + 1) * piece)
+        return part[slot, core, 0, at].astype(F32) + sib_in[slot, 0, at].astype(F32) + x_in[slot, at].astype(F32)
+
+    def pass_on(way, k, chunk, incoming):
+        value = local_sum(k, chunk)
+        if incoming:
+            index = k if way == 1 else 8 - k
+            return_z(way, k + 1 if way == 1 else k - 1, chunk).wait_recv()
+            value = value + z_in[way, index, chunk].astype(F32)
+        copy = return_z(way, k, chunk)
+        k_dst = k - 1 if way == 1 else (k + 1) % 8
+        z_out[way, k_dst if way == 1 else (8 - k_dst) % 8, chunk] = value.astype(BF16)
+        copy.start()
+
+    def settle(step):
+        for slot in slots[step]:
+            return_x(slot).wait_recv()
+
+    settle(4)
+    pass_on(1, 4, 0, False)
+    pass_on(0, 4, 1, False)
+    settle(3)
+    pass_on(1, 3, 1, False)
+    pass_on(0, 5, 0, False)
+    pass_on(1, 3, 0, True)
+    pass_on(0, 5, 1, True)
+    settle(2)
+    for chunk in (1, 0):
+        pass_on(1, 2, chunk, True)
+        pass_on(0, 6, 1 - chunk, True)
+    settle(1)
+    for chunk in (1, 0):
+        pass_on(1, 1, chunk, True)
+        pass_on(0, 7, 1 - chunk, True)
+    settle(0)
+    for chunk in (1, 0):
+        return_z(1, 1, chunk).wait_recv()
+        return_z(0, 7, chunk).wait_recv()
+        at = slice(chunk * piece, (chunk + 1) * piece)
+        combined = local_sum(0, chunk) + z_in[1, 0, chunk].astype(F32) + z_in[0, 0, chunk].astype(F32)
+        out_ref[at] = (after[at].astype(F32) + routed_factor * combined).astype(BF16)
+
+    for copy in head_copies + y_copies:
+        copy.wait_send()
+    for step in (1, 2, 3, 4):
+        for way in (0, 1):
+            for chunk in (0, 1):
+                if step < 4 or chunk == way:
+                    gather_z(way, step, chunk).wait_send()
+                if step < 4 or chunk != way:
+                    return_z(way, step if way == 1 else 8 - step, chunk).wait_send()
+    for k in range(8):
+        gather_x(k).wait_send()
+        gather_s(k, 0, core).wait_send()
+        gather_s(k, 1, core).wait_send()
+        return_s(k, 1 - core).wait_send()
+        return_x(k).wait_send()
+
+
+def finish_layer(head_out, w_out_part, resid, gain, share, gate, up, down):
+    count, width = resid.shape
+    units, values = gate.shape[1], head_out.shape[1]
+    heads = head_out.reshape(2, 4, 2, count, values)
+    dma = pltpu.SemaphoreType.DMA
+    vmem = pl.BlockSpec(memory_space=pltpu.VMEM)
+    hbm = pl.BlockSpec(memory_space=pl.ANY)
+    return pl.pallas_call(
+        layer_kernel,
+        out_shape=jax.ShapeDtypeStruct((count, width), BF16),
+        in_specs=[vmem, hbm, vmem, vmem, vmem, hbm, hbm, hbm],
+        out_specs=vmem,
+        scratch_shapes=[
+            pltpu.VMEM(w_out_part.shape, BF16),
+            pltpu.VMEM((width, units), BF16),
+            pltpu.VMEM((width, units), BF16),
+            pltpu.VMEM((width, units), BF16),
+            pltpu.VMEM((4, 4, count, values), BF16),
+            pltpu.VMEM((4, count, width), F32),
+            pltpu.VMEM((4, count, width), BF16),
+            pltpu.VMEM((3, count, width), BF16),
+            pltpu.VMEM((count, width), BF16),
+            pltpu.VMEM((8, 2, 2, count, width + 128), BF16),
+            pltpu.VMEM((8, 2, 2, count, width), BF16),
+            pltpu.VMEM((8, 2, count, width), BF16),
+            pltpu.VMEM((8, count, width), BF16),
+            pltpu.VMEM((8, count, width), BF16),
+            pltpu.VMEM((2, 4, 2, count // 2, width), BF16),
+            pltpu.VMEM((2, 4, 2, count // 2, width), BF16),
+            dma((4,)), dma((3,)), dma((3,)), dma((3,)), dma((3,)),
+            dma((2, 4, 2)), dma((2, 4, 2)), dma((8,)), dma((8,)), dma((2, 8)), dma((2, 8)),
+            dma((8,)), dma((8,)), dma((8,)), dma((8,)), dma((2, 4, 2)), dma((2, 4, 2)),
+        ],
+        name="layer",
+        compiler_params=pltpu.CompilerParams(collective_id=1, has_side_effects=True, vmem_limit_bytes=60 << 20),
+    )(heads, w_out_part, resid, gain.reshape(1, width), share, gate, up, down)
+
+
+def routing_shares(expert_ids, route_scores, experts):
+    combine = route_scores / jnp.sum(route_scores, axis=1, keepdims=True)
+    named = expert_ids[:, :, None] == jnp.arange(experts, dtype=jnp.int32)[None, None, :]
+    dense = jnp.sum(jnp.where(named, combine[:, :, None], 0.0), axis=1)
+    coarse = lax.reduce_precision(dense, 8, 7)
+    pieces = jnp.concatenate([coarse, dense - coarse], axis=1).astype(BF16)
+    return jnp.pad(pieces, ((0, 0), (0, 128 - 2 * experts)))
 
 
 def per_device(
@@ -336,52 +591,13 @@
     expert_ids,
     route_scores,
 ):
-    tokens_here = q_latent.shape[0]
-    heads_here = q_latent.shape[1]
-    latent_width = w_value.shape[1]
-    width = resid.shape[1]
-    rows = resid.shape[0]
-    head_out, _ = attend(q_latent.reshape(tokens_here, q_latent.shape[2]), kv_latent, w_value[0], w_out)
-    head_out = head_out.reshape(tokens_here, 1, w_value.shape[2])
-    grouped = lax.all_to_all(head_out, ("head", "ep"), split_axis=0, concat_axis=1, tiled=True)
-    flat_heads = grouped.reshape(rows, grouped.shape[1] * grouped.shape[2])
-    attended = make_projection(
-        flat_heads, lax.all_gather(w_out, ("head", "ep"), axis=0, tiled=True)
+    head_out, w_out_part = attend(
+        q_latent.reshape(q_latent.shape[0], q_latent.shape[2]), kv_latent, w_value[0], w_out
     )
-    after_attn = lax.optimization_barrier(
-        (resid.astype(jnp.float32) + attended).astype(jnp.bfloat16)
+    share = routing_shares(expert_ids, route_scores, lax.axis_size("ctx"))
+    return finish_layer(
+        head_out, w_out_part, resid, norm_gain, share, w_gate[0], w_up[0], w_down_t[0]
     )
-    widened = after_attn.astype(jnp.float32)
-    mean_square = jnp.mean(widened * widened, axis=1, keepdims=True)
-    normed = (widened * lax.rsqrt(mean_square + norm_epsilon) * norm_gain).astype(jnp.bfloat16)
-    experts_here = lax.axis_size("ctx")
-    capacity = 5 * rows * TOPK // (4 * experts_here)
-    chosen = expert_ids.reshape(rows * TOPK)
-    onehot = (chosen[:, None] == jnp.arange(experts_here, dtype=jnp.int32)[None, :]).astype(
-        jnp.int32
-    )
-    ranking = jnp.sum(onehot * (jnp.cumsum(onehot, axis=0) - 1), axis=1)
-    slot_ids = chosen * capacity + ranking
-    slot_table = jnp.arange(experts_here * capacity, dtype=jnp.int32)
-    placing = jnp.any(slot_ids.reshape(rows, TOPK)[None, :, :] == slot_table[:, None, None], axis=2)
-    dispatch = jnp.dot(
-        placing.astype(jnp.bfloat16), normed, preferred_element_type=jnp.float32
-    ).astype(jnp.bfloat16)
-    dispatch = dispatch.reshape(experts_here, capacity, width)
-    arrived = lax.all_to_all(dispatch, "ctx", split_axis=0, concat_axis=0, tiled=True)
-    pooled = lax.all_gather(arrived, "head", axis=0, tiled=True).reshape(-1, width)
-    produced = lax.psum_scatter(
-        expert_half(pooled, w_gate[0], w_up[0], w_down_t[0]).astype(jnp.bfloat16),
-        "head",
-        scatter_dimension=0,
-        tiled=True,
-    )
-    outgoing = produced.reshape(experts_here, capacity, width)
-    returned = lax.all_to_all(outgoing, "ctx", split_axis=0, concat_axis=0, tiled=True)
-    picked = returned.reshape(experts_here * capacity, width)[slot_ids].reshape(rows, TOPK, width)
-    combine = route_scores / jnp.sum(route_scores, axis=1, keepdims=True)
-    combined = jnp.sum(picked.astype(jnp.float32) * combine[:, :, None], axis=1)
-    return (widened + routed_factor * combined).astype(jnp.bfloat16)
 
 
 def solution(mesh):

time: 248 us -> 144 us (0.58)
  waiting for transfers between devices: 61.7 us -> 0 us
  Pallas kernels: 64.6 us -> 123 us
  blocking collectives: 33.6 us -> 0 us
  starting transfers between devices: 20.7 us -> 0 us
  matrix products: 19.1 us -> 0 us
  between operations: 13.3 us -> 0.04 us
  local copies, waits for them, and re-layouts: 28 us -> 16.5 us
  other arithmetic: 5.66 us -> 2.97 us
    pallas_call x0 -> x1, Pallas kernels: none -> 71.3 us  [finish_layer(): pl.pallas_call(layer_kernel, out_shape=jax.ShapeDtypeStruct((count, width...]
    all_to_all x1 -> x0, blocking collectives: 33.6 us -> none  [per_device(): lax.all_to_all(dispatch, 'ctx', split_axis=0, concat_axis=0, tiled=True)]
    all_to_all x2 -> x0, waiting for transfers between devices: 32.8 us -> none  [the longest x1 26.1 us: per_device(): lax.all_to_all(outgoing, 'ctx', split_axis=0, concat_axis=0, tiled=True)]
    all_to_all x2 -> x0, starting transfers between devices: 20.4 us -> none  [the longest x1 11.9 us: per_device(): lax.all_to_all(head_out, ('head', 'ep'), split_axis=0, concat_axis=1, til...]
    dot_general x4 -> x0, matrix products: 19.1 us -> none  [the longest x1 7.46 us: expert_half(): lax.dot_general(hidden, down_part, (((1,), (1,)), ((), ())), preferred_el...]
    reduce_scatter x1 -> x0, waiting for transfers between devices: 16.2 us -> none  [per_device(): lax.psum_scatter(expert_half(pooled, w_gate[0], w_up[0], w_down_t[0]).ast...]
    pallas_call x1, Pallas kernels: 64.6 us -> 52.2 us  [attend(): pl.pallas_call(attention_kernel, out_shape=(jax.ShapeDtypeStruct((tokens,...]
    unnamed x18 -> x10, local copies, waits for them, and re-layouts: 4.25 us -> 16.3 us
  transfers between devices with their start and end apart: 5 -> 0, of which waited for: 4 -> 0; matrix products, arithmetic and copies ran while one was open for 3% -> 0% of each run, Pallas kernels for 26% -> 0%
where the time goes in v2:
time: 144 us; the launch traced here: 143 us
  Pallas kernels  123 us (85%)
  local copies, waits for them, and re-layouts  16.5 us (11%)
  other arithmetic  2.97 us (2%)
    pallas_call x1, Pallas kernels, finish_layer(): pl.pallas_call(layer_kernel, out_shape=jax.ShapeDtypeStruct((count, width...  71.3 us
    pallas_call x1, Pallas kernels, attend(): pl.pallas_call(attention_kernel, out_shape=(jax.ShapeDtypeStruct((tokens,...  52.2 us
    unnamed x10, local copies, waits for them, and re-layouts  16.3 us

profile of v2, /device:TPU:2, one launch (start us, length us, event | category | flops | bytes accessed | tf_op | source)
XLA Modules:
  0.0 143.0 jit_solution(8008333080892531269)
XLA Ops:
  0.0 0.0 copy-start
  0.0 0.9 reduce_sum.18
  0.9 0.7 broadcast_divide_fusion
  1.6 0.7 select_reduce_fusion
  2.3 0.1 copy.29
  2.4 0.1 copy.28
  2.4 0.7 fusion.2.share_ref
  3.1 2.1 %copy.26 = bf16[512,1,576]{2,0,1:T(8,128)(2,1)} copy(bf16[512,1,576]{0,2,1:T(8,128)(2,1)} %param.11) | data formatting | bytes 1179648 | tf_op args[0]
  5.3 2.2 %copy.27.kv_ref = bf16[512,576]{1,0:T(8,128)(2,1)} copy(bf16[512,576]{0,1:T(8,128)(2,1)} %param.12) | data formatting | bytes 1179648 | tf_op args[1]
  7.4 52.2 %attention.1 = (bf16[512,128]{1,0:T(8,128)(2,1)}, bf16[4,128,2048]{2,1,0:T(8,128)(2,1)}) custom-call(bf16[512,576]{1,0:T(8,128)(2,1)} %bitcast.10, bf16[512,576]{1,0:T(8,128)(2,1)} %copy.27.kv_ref, bf16[512,128]{1,0:T(8,128)(2,1)} %bitcast.12, bf16[128,2048]{1,0:T(8,128)(2,1)} %wo_ref.1), custom_call_target="tpu_custom_call" | custom-call | tf_op jit(solution)/shard_map/attention/pallas_call | solution.py:286
  59.6 0.0 copy-done
  59.6 2.8 %copy.31 = bf16[1,2048,704]{2,1,0:T(8,128)(2,1)} copy(bf16[1,2048,704]{1,2,0:T(8,128)(2,1)S(1)} %copy-done) | data formatting | bytes 5767168 | tf_op args[6]
  62.4 0.0 copy-start.1
  62.4 4.8 %copy.32 = bf16[1,2048,704]{2,1,0:T(8,128)(2,1)} copy(bf16[1,2048,704]{1,2,0:T(8,128)(2,1)} %param.18) | data formatting | bytes 5767168 | tf_op args[7]
  67.2 0.0 copy-done.1
  67.2 2.9 %copy.33 = bf16[1,2048,704]{2,1,0:T(8,128)(2,1)} copy(bf16[1,2048,704]{1,2,0:T(8,128)(2,1)S(1)} %copy-done.1) | data formatting | bytes 5767168 | tf_op args[8]
  70.1 71.3 %layer.1 = bf16[32,2048]{1,0:T(8,128)(2,1)} custom-call(bf16[2,4,2,32,128]{4,3,2,1,0:T(8,128)(2,1)} %bitcast.11, bf16[4,128,2048]{2,1,0:T(8,128)(2,1)} %get-tuple-element.8.wo_ref, bf16[32,2048]{1,0:T(8,128)(2,1)} %resid_ref.1, f32[1,2048]{1,0:T(1,128)} %bitcast.13, bf16[32,128]{1,0:T(8,128)(2,1)} %fusion.2.share_ref, bf16[2048,704]{1,0:T(8,128)(2,1)} %bitcast.7, ...), custom_call_target="tpu_custom_call" | custom-call | tf_op jit(solution)/shard_map/layer/pallas_call | solution.py:541
  141.4 1.6 %copy.35 = bf16[32,2048]{1,0:T(8,128)(2,1)} copy(bf16[32,2048]{1,0:T(8,128)(2,1)} %layer.1) | data formatting | bytes 262144
  (2 shorter events, 0.0 us)
Async XLA Ops:
  0.0 59.6 %copy-start = (bf16[1,2048,704]{1,2,0:T(8,128)(2,1)S(1)}, bf16[1,2048,704]{1,2,0:T(8,128)(2,1)}, u32[]{:S(2)}) copy-start(bf16[1,2048,704]{1,2,0:T(8,128)(2,1)} %param.17) | copy-start | bytes 8650756
  62.4 4.8 %copy-start.1 = (bf16[1,2048,704]{1,2,0:T(8,128)(2,1)S(1)}, bf16[1,2048,704]{1,2,0:T(8,128)(2,1)}, u32[]{:S(2)}) copy-start(bf16[1,2048,704]{1,2,0:T(8,128)(2,1)} %param.19) | copy-start | bytes 8650756

commit v3 on v2

--- a/solution.py
+++ b/solution.py
@@ -53,14 +53,14 @@
 
 def attention_kernel(
     q_ref, kv_ref, wv_ref, wo_ref, out_ref, wo4_ref,
-    keys, q_far, wv_far, high, denom, accum, back, back_lse, far_out, far_lse,
+    keys, q_far, queries, wv_far, high, denom, accum, back, back_lse, far_out, far_lse,
     z_send, z_recv, y_send, y_recv, s_send, s_recv, q_send, q_recv, w_send, w_recv, own_sem,
 ):
     x, y, z, core = coords()
     x_lo, x_hi, parity = x % 2, x // 2, y % 2
-    tokens, latent = q_ref.shape[0], wv_ref.shape[0]
-    half, quarter = tokens // 2, tokens // 4
-    z_up, z_down = device(x, y, z + 1, core), device(x, y, z - 1, core)
+    tokens, latent = q_ref.shape[1], wv_ref.shape[0]
+    half, quarter, piece = tokens // 2, tokens // 4, q_ref.shape[0] // 2
+    z_way = (device(x, y, z + 1, core), device(x, y, z - 1, core))
     y_up, y_down = device(x, y + 1, z, core), device(x, y - 1, z, core)
     x_up, x_down = device(x + 1, y, z, core), device(x - 1, y, z, core)
     sibling = device(x, y, z, 1 - core)
@@ -69,48 +69,42 @@
     x_from = device(x + 1 - 2 * core, y, z, core)
     x_other = device(x - 1 + 2 * x_lo, y, z, core)
 
-    row_mine = parity * half + core * quarter
-    row_other = (1 - parity) * half + core * quarter
-    row_sib_mine = parity * half + (1 - core) * quarter
-    row_sib_other = (1 - parity) * half + (1 - core) * quarter
-
-    def rows(k, start, size):
-        return keys.at[pl.ds(pl.multiple_of(SLOT[k] * tokens + start, 16), size)]
-
-    def z_copy(way, step):
-        target = z_up if way == 0 else z_down
+    mine, other = parity * 2 + core, (1 - parity) * 2 + core
+    sib_mine, sib_other = parity * 2 + 1 - core, (1 - parity) * 2 + 1 - core
+
+    def z_copy(way, step, chunk):
         k_dst = step if way == 0 else 8 - step
-        k_src = step - 1 if way == 0 else (8 - (step - 1)) % 8
-        start, size = row_mine, quarter
-        if step == 4:
-            size = quarter // 2
-            start = row_mine + way * size
-        if k_src == 0:
-            src = kv_ref.at[pl.ds(pl.multiple_of(start, 16), size)]
-        else:
-            src = rows(k_src, start, size)
-        return remote(src, rows(k_dst, start, size), z_send.at[way, step - 1], z_recv.at[way, step - 1], target)
-
-    def y_copy(k, start):
-        return remote(rows(k, start, quarter), rows(k, start, quarter), y_send.at[k - 1], y_recv.at[k - 1], y_to)
-
-    def s_copy(k, which, start):
-        return remote(rows(k, start, quarter), rows(k, start, quarter), s_send.at[which, k - 1], s_recv.at[which, k - 1], sibling)
+        k_src = step - 1 if way == 0 else (9 - step) % 8
+        at = pl.ds(chunk * piece, piece)
+        return remote(
+            keys.at[SLOT[k_src], mine, at], keys.at[SLOT[k_dst], mine, at],
+            z_send.at[way, step - 1, chunk], z_recv.at[way, step - 1, chunk], z_way[way])
+
+    def y_copy(k, which):
+        at = keys.at[SLOT[k], which]
+        return remote(at, at, y_send.at[k - 1], y_recv.at[k - 1], y_to)
+
+    def s_copy(k, row, which):
+        at = keys.at[SLOT[k], which]
+        return remote(at, at, s_send.at[row, k - 1], s_recv.at[row, k - 1], sibling)
 
     q_copy = remote(q_ref, q_far, q_send.at[0], q_recv.at[0], x_to)
     wv_copy = remote(wv_ref, wv_far, q_send.at[1], q_recv.at[1], x_to)
     back_copy = remote(back, far_out, q_send.at[2], q_recv.at[2], x_from)
     lse_copy = remote(back_lse, far_lse, q_send.at[3], q_recv.at[3], x_from)
-    mine, partner = core * 2 + x_hi, core * 2 + 1 - x_hi
-    wo_own = pltpu.make_async_copy(wo_ref, wo4_ref.at[mine], own_sem)
-    wo_sib = remote(wo_ref, wo4_ref.at[mine], w_send.at[0], w_recv.at[0], sibling)
-    wo_far = remote(wo_ref, wo4_ref.at[mine], w_send.at[1], w_recv.at[1], x_other)
+    place, partner = core * 2 + x_hi, core * 2 + 1 - x_hi
+    wo_own = pltpu.make_async_copy(wo_ref, wo4_ref.at[place], own_sem)
+    wo_sib = remote(wo_ref, wo4_ref.at[place], w_send.at[0], w_recv.at[0], sibling)
+    wo_far = remote(wo_ref, wo4_ref.at[place], w_send.at[1], w_recv.at[1], x_other)
     wo_fwd = remote(wo4_ref.at[partner], wo4_ref.at[partner], w_send.at[2], w_recv.at[2], sibling)
 
-    greet([z_up, z_down, y_up, y_down, x_up, x_down, sibling])
-
-    z_copy(0, 1).start()
-    z_copy(1, 1).start()
+    for j in range(4):
+        keys[0, j] = kv_ref[:, j * quarter:(j + 1) * quarter]
+    greet([*z_way, y_up, y_down, x_up, x_down, sibling])
+
+    for chunk in (0, 1):
+        for way in (0, 1):
+            z_copy(way, 1, chunk).start()
 
     @pl.when(x_lo == 1)
     def _():
@@ -121,15 +115,15 @@
     wo_sib.start()
     wo_far.start()
 
-    keys[0:tokens] = kv_ref[...]
+    queries[0] = q_ref[...].T
     high[...] = jnp.full(high.shape, masked_score, F32)
     denom[...] = jnp.zeros(denom.shape, F32)
     accum[...] = jnp.zeros(accum.shape, F32)
 
-    def tile(which, queries, slot, count, change=None):
-        block = keys[slot * tokens:(slot + count) * tokens]
+    def tile(which, slot, count, change=None):
+        block = jnp.concatenate([keys[slot + i, j] for i in range(count) for j in range(4)], axis=1)
         chunks = [slice(0, half), slice(half, tokens)]
-        scores = [dot(queries[rows_at], block, NT) for rows_at in chunks]
+        scores = [dot(queries[which, rows_at], block) for rows_at in chunks]
         for rows_at, score in zip(chunks, scores):
             if change is not None:
                 score = change(score, rows_at.start)
@@ -140,7 +134,7 @@
             weight = jnp.exp2((score - new) * EXP_SCALE)
             denom[at] = denom[at] * keep + jnp.sum(weight, axis=1, keepdims=True)
             high[at] = new
-            accum[at] = accum[at] * keep + dot(weight.astype(BF16), block[:, :latent])
+            accum[at] = accum[at] * keep + dot(weight.astype(BF16), block[:latent], NT)
 
     def diagonal(score, start):
         row = start + lax.broadcasted_iota(jnp.int32, score.shape, 0)
@@ -161,66 +155,77 @@
 
         @pl.when(both)
         def _():
-            tile(0, q_ref, SLOT[step], 2)
+            tile(0, SLOT[step], 2)
 
         @pl.when(some & jnp.logical_not(both))
         def _():
-            tile(0, q_ref, SLOT[step], 2, pair_mask(step))
+            tile(0, SLOT[step], 2, pair_mask(step))
 
     def far_tile(slot, count):
         @pl.when(x_lo == 0)
         def _():
-            tile(1, q_far, slot, count)
-
-    tile(0, q_ref, 0, 1, diagonal)
-
-    def after_z(step):
-        ks = [step, 8 - step] if step < 4 else [4]
-        z_copy(0, step).wait_recv()
-        z_copy(1, step).wait_recv()
-        if step < 4:
-            z_copy(0, step + 1).start()
-            z_copy(1, step + 1).start()
-        for k in ks:
-            y_copy(k, row_mine).start()
-            s_copy(k, 0, row_mine).start()
+            tile(1, slot, count)
+
+    members = {1: [1, 7], 2: [2, 6], 3: [3, 5], 4: [4]}
+
+    def after_z(step, chunk):
+        for way in (0, 1):
+            if step < 4 or chunk == way:
+                z_copy(way, step, chunk).wait_recv()
+                if step < 3 or (step == 3 and chunk == way):
+                    z_copy(way, step + 1, chunk).start()
+
+    def share_z(step):
+        for k in members[step]:
+            y_copy(k, mine).start()
+            s_copy(k, 0, mine).start()
 
     def after_y(step):
-        for k in ([step, 8 - step] if step < 4 else [4]):
-            y_copy(k, row_other).wait_recv()
-            s_copy(k, 1, row_other).start()
+        for k in members[step]:
+            y_copy(k, other).wait_recv()
+            s_copy(k, 1, other).start()
 
     def after_s(step):
-        for k in ([step, 8 - step] if step < 4 else [4]):
-            s_copy(k, 0, row_sib_mine).wait_recv()
-            s_copy(k, 1, row_sib_other).wait_recv()
-
-    after_z(1)
-    after_y(1)
+        for k in members[step]:
+            s_copy(k, 0, sib_mine).wait_recv()
+            s_copy(k, 1, sib_other).wait_recv()
+
+    tile(0, 0, 1, diagonal)
+    after_z(1, 0)
+    after_z(1, 1)
+    share_z(1)
 
     @pl.when(x_lo == 0)
     def _():
         q_copy.wait_recv()
         wv_copy.wait_recv()
-
+        queries[1] = q_far[...].T
+
+    after_z(2, 0)
+    after_y(1)
     far_tile(0, 1)
-    after_z(2)
+    after_z(2, 1)
+    share_z(2)
     after_s(1)
     own_pair(1)
+    after_z(3, 0)
     after_y(2)
     far_tile(1, 2)
-    after_z(3)
+    after_z(3, 1)
+    share_z(3)
     after_s(2)
     own_pair(2)
+    after_z(4, 0)
+    after_z(4, 1)
+    share_z(4)
     after_y(3)
     far_tile(3, 2)
-    after_z(4)
     after_s(3)
+    after_y(4)
     own_pair(3)
-    after_y(4)
-    far_tile(5, 2)
     wo_far.wait_recv()
     wo_fwd.start()
+    far_tile(5, 2)
     after_s(4)
     far_tile(7, 1)
 
@@ -235,7 +240,7 @@
 
     @pl.when(z >= 4)
     def _():
-        tile(0, q_ref, 7, 1)
+        tile(0, 7, 1)
 
     head_out = dot((accum[0] / denom[0]).astype(BF16), wv_ref[...])
 
@@ -248,9 +253,9 @@
         lse = high[0] * EXP_SCALE + jnp.log2(denom[0])
         back_copy.wait_recv()
         lse_copy.wait_recv()
-        other = jnp.broadcast_to(far_lse[0:1], (128, tokens)).T
-        top = jnp.maximum(lse, other)
-        near_part, far_part = jnp.exp2(lse - top), jnp.exp2(other - top)
+        far = jnp.broadcast_to(far_lse[0:1], (128, tokens)).T
+        top = jnp.maximum(lse, far)
+        near_part, far_part = jnp.exp2(lse - top), jnp.exp2(far - top)
         out_ref[...] = ((head_out * near_part + far_out[...].astype(F32) * far_part) / (near_part + far_part)).astype(BF16)
 
     wo_sib.wait_recv()
@@ -259,12 +264,14 @@
     for copy in (wo_sib, wo_far, wo_fwd):
         copy.wait_send()
     for step in range(1, 5):
-        z_copy(0, step).wait_send()
-        z_copy(1, step).wait_send()
+        for way in (0, 1):
+            for chunk in (0, 1):
+                if step < 4 or chunk == way:
+                    z_copy(way, step, chunk).wait_send()
     for k in range(1, 8):
-        y_copy(k, row_mine).wait_send()
-        s_copy(k, 0, row_mine).wait_send()
-        s_copy(k, 1, row_other).wait_send()
+        y_copy(k, mine).wait_send()
+        s_copy(k, 0, mine).wait_send()
+        s_copy(k, 1, other).wait_send()
 
     @pl.when(x_lo == 1)
     def _():
@@ -278,7 +285,7 @@
 
 
 def attend(queries, kv, w_value, w_out):
-    tokens, width = queries.shape
+    width, tokens = queries.shape
     latent, values = w_value.shape
     dma = pltpu.SemaphoreType.DMA
     vmem = pl.BlockSpec(memory_space=pltpu.VMEM)
@@ -292,8 +299,9 @@
         in_specs=[vmem, vmem, vmem, hbm],
         out_specs=(vmem, hbm),
         scratch_shapes=[
-            pltpu.VMEM((8 * tokens, width), BF16),
-            pltpu.VMEM((tokens, width), BF16),
+            pltpu.VMEM((8, 4, width, tokens // 4), BF16),
+            pltpu.VMEM((width, tokens), BF16),
+            pltpu.VMEM((2, tokens, width), BF16),
             pltpu.VMEM((latent, values), BF16),
             pltpu.VMEM((2, tokens, 1), F32),
             pltpu.VMEM((2, tokens, 1), F32),
@@ -302,7 +310,7 @@
             pltpu.VMEM((8, tokens), F32),
             pltpu.VMEM((tokens, values), BF16),
             pltpu.VMEM((8, tokens), F32),
-            dma((2, 4)), dma((2, 4)), dma((7,)), dma((7,)), dma((2, 7)), dma((2, 7)),
+            dma((2, 4, 2)), dma((2, 4, 2)), dma((7,)), dma((7,)), dma((2, 7)), dma((2, 7)),
             dma((4,)), dma((4,)), dma((3,)), dma((3,)), dma,
         ],
         name="attention",
@@ -310,9 +318,21 @@
     )(queries, kv, w_value, w_out)
 
 
+def routing_shares(ids_ref, scores_ref, experts):
+    scores = scores_ref[...]
+    combine = scores / jnp.sum(scores, axis=0, keepdims=True)
+    lane = lax.broadcasted_iota(jnp.int32, (128, scores.shape[1]), 0)
+    dense = jnp.zeros((128, scores.shape[1]), F32)
+    for k in range(scores.shape[0]):
+        chosen = ids_ref[k:k + 1]
+        dense += jnp.where((lane == chosen) | (lane == chosen + experts), combine[k:k + 1], 0.0)
+    coarse = dense.astype(BF16).astype(F32)
+    return jnp.where(lane < experts, coarse, dense - coarse).T
+
+
 def layer_kernel(
-    heads_ref, wo_ref, resid_ref, gain_ref, share_ref, gate_ref, up_ref, down_ref, out_ref,
-    wo, gate, up, down, pool, proj, proj_out, y_in, after, rows_in, part, sib_in, x_out, x_in,
+    heads_ref, wo_ref, resid_ref, gain_ref, ids_ref, scores_ref, gate_ref, up_ref, down_ref, out_ref,
+    wo, gate, up, down, pool, proj, proj_out, y_in, after, rows_in, part, hidden, sib_in, x_out, x_in,
     z_out, z_in,
     load_sem, h_send, h_recv, y_send, y_recv, az_send, az_recv, ax_send, ax_recv, as_send, as_recv,
     bs_send, bs_recv, bx_send, bx_recv, bz_send, bz_recv,
@@ -368,7 +388,7 @@
     mean_square = jnp.mean(widened * widened, axis=1, keepdims=True)
     normed = (widened * lax.rsqrt(mean_square + norm_epsilon) * gain_ref[...]).astype(BF16)
     rows_in[0, core, 0, :, 0:width] = normed
-    rows_in[0, core, 0, :, width:] = share_ref[...]
+    rows_in[0, core, 0, :, width:] = routing_shares(ids_ref, scores_ref, 16).astype(BF16)
 
     def gather_z(way, step, chunk):
         k_dst = step if way == 0 else 8 - step
@@ -401,19 +421,21 @@
     members = [[0], [1, 7], [2, 6], [3, 5], [4]]
     slots = [[SLOT[k] for k in ks] for ks in members]
 
-    def experts(step):
+    def hidden_units(step):
         first, number = slots[step][0], len(slots[step])
         block = rows_in[first:first + number].reshape(number * 4 * count, rows_in.shape[4])
         source, shares = block[:, :width], block[:, width:].astype(F32)
         lane = lax.broadcasted_iota(jnp.int32, shares.shape, 1)
         expert = lax.axis_index("ctx")
         share = jnp.sum(jnp.where((lane == expert) | (lane == expert + 16), shares, 0.0), axis=1, keepdims=True)
-        gated = dot(source, gate[...])
-        hidden = (gated / (1.0 + jnp.exp(-gated)) * dot(source, up[...]) * share).astype(BF16)
-        made = dot(hidden, down[...], NT).astype(BF16)
+        gated = dot(source, gate[...], NT)
+        value = gated / (1.0 + jnp.exp(-gated)) * dot(source, up[...], NT) * share
+        hidden[0:number * 4 * count] = value.astype(BF16)
+
+    def project_down(step):
+        first, number = slots[step][0], len(slots[step])
+        made = dot(hidden[0:number * 4 * count], down[...]).astype(BF16)
         part[first:first + number] = made.reshape(number, 2, 2, count, width)
-
-    def send_parts(step):
         for slot in slots[step]:
             return_s(slot, 1 - core).start()
 
@@ -423,14 +445,14 @@
             x_out[slot] = (part[slot, core, 1].astype(F32) + sib_in[slot, 1].astype(F32)).astype(BF16)
             return_x(slot).start()
 
-    def after_z(step):
-        for chunk in (0, 1):
-            for way in (0, 1):
-                if step == 4 and chunk != way:
-                    continue
+    def after_z(step, chunk):
+        for way in (0, 1):
+            if step < 4 or chunk == way:
                 gather_z(way, step, chunk).wait_recv()
                 if step < 3 or (step == 3 and chunk == way):
                     gather_z(way, step + 1, chunk).start()
+
+    def share_z(step):
         for k in members[step]:
             gather_x(k).start()
             gather_s(k, 0, core).start()
@@ -452,24 +474,42 @@
     gather_s(0, 0, core).start()
     for load in loads[1:]:
         load.wait()
+    after_z(1, 0)
+    after_z(1, 1)
+    share_z(1)
     after_x(0)
     after_s(0)
-    experts(0)
-    send_parts(0)
-    for step in (1, 2, 3, 4):
-        after_z(step)
-        if step > 1:
-            after_x(step - 1)
-            after_s(step - 1)
-            experts(step - 1)
-            send_parts(step - 1)
-            fold_siblings(step - 2)
+    hidden_units(0)
+    after_z(2, 0)
+    project_down(0)
+    after_z(2, 1)
+    share_z(2)
+    after_x(1)
+    after_z(3, 0)
+    after_s(1)
+    fold_siblings(0)
+    hidden_units(1)
+    after_z(3, 1)
+    share_z(3)
+    project_down(1)
+    after_z(4, 0)
+    after_z(4, 1)
+    share_z(4)
+    after_x(2)
+    after_s(2)
+    hidden_units(2)
+    after_x(3)
+    fold_siblings(1)
+    project_down(2)
+    after_s(3)
+    hidden_units(3)
     after_x(4)
+    fold_siblings(2)
+    project_down(3)
     after_s(4)
-    experts(4)
-    send_parts(4)
+    hidden_units(4)
     fold_siblings(3)
-    fold_siblings(4)
+    project_down(4)
 
     def local_sum(k, chunk):
         slot, at = SLOT[k], slice(chunk * piece, (chunk + 1) * piece)
@@ -490,12 +530,13 @@
         for slot in slots[step]:
             return_x(slot).wait_recv()
 
+    settle(3)
+    pass_on(1, 3, 1, False)
+    pass_on(0, 5, 0, False)
+    fold_siblings(4)
     settle(4)
     pass_on(1, 4, 0, False)
     pass_on(0, 4, 1, False)
-    settle(3)
-    pass_on(1, 3, 1, False)
-    pass_on(0, 5, 0, False)
     pass_on(1, 3, 0, True)
     pass_on(0, 5, 1, True)
     settle(2)
@@ -531,9 +572,9 @@
         return_x(k).wait_send()
 
 
-def finish_layer(head_out, w_out_part, resid, gain, share, gate, up, down):
+def finish_layer(head_out, w_out_part, resid, gain, ids, scores, gate, up, down):
     count, width = resid.shape
-    units, values = gate.shape[1], head_out.shape[1]
+    units, values = gate.shape[0], head_out.shape[1]
     heads = head_out.reshape(2, 4, 2, count, values)
     dma = pltpu.SemaphoreType.DMA
     vmem = pl.BlockSpec(memory_space=pltpu.VMEM)
@@ -541,13 +582,13 @@
     return pl.pallas_call(
         layer_kernel,
         out_shape=jax.ShapeDtypeStruct((count, width), BF16),
-        in_specs=[vmem, hbm, vmem, vmem, vmem, hbm, hbm, hbm],
+        in_specs=[vmem, hbm, vmem, vmem, vmem, vmem, hbm, hbm, hbm],
         out_specs=vmem,
         scratch_shapes=[
             pltpu.VMEM(w_out_part.shape, BF16),
-            pltpu.VMEM((width, units), BF16),
-            pltpu.VMEM((width, units), BF16),
-            pltpu.VMEM((width, units), BF16),
+            pltpu.VMEM((units, width), BF16),
+            pltpu.VMEM((units, width), BF16),
+            pltpu.VMEM((units, width), BF16),
             pltpu.VMEM((4, 4, count, values), BF16),
             pltpu.VMEM((4, count, width), F32),
             pltpu.VMEM((4, count, width), BF16),
@@ -555,6 +596,7 @@
             pltpu.VMEM((count, width), BF16),
             pltpu.VMEM((8, 2, 2, count, width + 128), BF16),
             pltpu.VMEM((8, 2, 2, count, width), BF16),
+            pltpu.VMEM((8 * count, units), BF16),
             pltpu.VMEM((8, 2, count, width), BF16),
             pltpu.VMEM((8, count, width), BF16),
             pltpu.VMEM((8, count, width), BF16),
@@ -566,16 +608,7 @@
         ],
         name="layer",
         compiler_params=pltpu.CompilerParams(collective_id=1, has_side_effects=True, vmem_limit_bytes=60 << 20),
-    )(heads, w_out_part, resid, gain.reshape(1, width), share, gate, up, down)
-
-
-def routing_shares(expert_ids, route_scores, experts):
-    combine = route_scores / jnp.sum(route_scores, axis=1, keepdims=True)
-    named = expert_ids[:, :, None] == jnp.arange(experts, dtype=jnp.int32)[None, None, :]
-    dense = jnp.sum(jnp.where(named, combine[:, :, None], 0.0), axis=1)
-    coarse = lax.reduce_precision(dense, 8, 7)
-    pieces = jnp.concatenate([coarse, dense - coarse], axis=1).astype(BF16)
-    return jnp.pad(pieces, ((0, 0), (0, 128 - 2 * experts)))
+    )(heads, w_out_part, resid, gain.reshape(1, width), ids, scores, gate, up, down)
 
 
 def per_device(
@@ -592,11 +625,10 @@
     route_scores,
 ):
     head_out, w_out_part = attend(
-        q_latent.reshape(q_latent.shape[0], q_latent.shape[2]), kv_latent, w_value[0], w_out
+        q_latent.reshape(q_latent.shape[0], q_latent.shape[2]).T, kv_latent.T, w_value[0], w_out
     )
-    share = routing_shares(expert_ids, route_scores, lax.axis_size("ctx"))
     return finish_layer(
-        head_out, w_out_part, resid, norm_gain, share, w_gate[0], w_up[0], w_down_t[0]
+        head_out, w_out_part, resid, norm_gain, expert_ids.T, route_scores.T, w_gate[0].T, w_up[0].T, w_down_t[0].T
     )
 
 

time: 144 us -> 123 us (0.85)
  local copies, waits for them, and re-layouts: 16.5 us -> 1.57 us
  other arithmetic: 2.97 us -> 0 us
  Pallas kernels: 123 us -> 121 us
    unnamed x10 -> x1, local copies, waits for them, and re-layouts: 16.3 us -> 1.57 us
    pallas_call x1, Pallas kernels: 52.2 us -> 47.1 us  [attend(): pl.pallas_call(attention_kernel, out_shape=(jax.ShapeDtypeStruct((tokens,...]
    pallas_call x1, Pallas kernels: 71.3 us -> 73.7 us  [finish_layer(): pl.pallas_call(layer_kernel, out_shape=jax.ShapeDtypeStruct((count, width...]
    reduce_sum x2 -> x0, other arithmetic: 1.56 us -> none  [the longest x1 0.85 us: routing_shares(): combine = route_scores / jnp.sum(route_scores, axis=1, keepdims=True)]
where the time goes in v3:
time: 123 us; the launch traced here: 122 us
  Pallas kernels  121 us (98%)
  local copies, waits for them, and re-layouts  1.57 us (1%)
    pallas_call x1, Pallas kernels, finish_layer(): pl.pallas_call(layer_kernel, out_shape=jax.ShapeDtypeStruct((count, width...  73.7 us
    pallas_call x1, Pallas kernels, attend(): pl.pallas_call(attention_kernel, out_shape=(jax.ShapeDtypeStruct((tokens,...  47.1 us

profile of v3, /device:TPU:2, one launch (start us, length us, event | category | flops | bytes accessed | tf_op | source)
XLA Modules:
  0.0 122.4 jit_solution(3801274977506315554)
XLA Ops:
  0.0 47.1 %attention.1 = (bf16[512,128]{1,0:T(8,128)(2,1)}, bf16[4,128,2048]{2,1,0:T(8,128)(2,1)}) custom-call(bf16[576,512]{1,0:T(8,128)(2,1)} %bitcast.21, bf16[576,512]{1,0:T(8,128)(2,1)} %bitcast.22, bf16[512,128]{1,0:T(8,128)(2,1)} %bitcast.24, bf16[128,2048]{1,0:T(8,128)(2,1)} %wo_ref.1), custom_call_target="tpu_custom_call" | custom-call | tf_op jit(solution)/shard_map/attention/pallas_call | solution.py:293
  47.1 73.7 %layer.1 = bf16[32,2048]{1,0:T(8,128)(2,1)} custom-call(bf16[2,4,2,32,128]{4,3,2,1,0:T(8,128)(2,1)} %bitcast.23, bf16[4,128,2048]{2,1,0:T(8,128)(2,1)} %get-tuple-element.8.wo_ref, bf16[32,2048]{1,0:T(8,128)(2,1)} %resid_ref.1, f32[1,2048]{1,0:T(1,128)} %bitcast.25, s32[6,32]{1,0:T(8,128)} %bitcast.26, f32[6,32]{1,0:T(8,128)} %bitcast.27, ...), custom_call_target="tpu_custom_call" | custom-call | tf_op jit(solution)/shard_map/layer/pallas_call | solution.py:582
  120.9 1.6 %copy.13 = bf16[32,2048]{1,0:T(8,128)(2,1)} copy(bf16[32,2048]{1,0:T(8,128)(2,1)} %layer.1) | data formatting | bytes 262144

commit v4 on v3

--- a/solution.py
+++ b/solution.py
@@ -51,8 +51,8 @@
 SLOT = {0: 0, 1: 1, 7: 2, 2: 3, 6: 4, 3: 5, 5: 6, 4: 7}
 
 
-def attention_kernel(
-    q_ref, kv_ref, wv_ref, wo_ref, out_ref, wo4_ref,
+def attention_part(
+    q_ref, kv_ref, wv_ref, wo_ref, heads, wo4_ref,
     keys, q_far, queries, wv_far, high, denom, accum, back, back_lse, far_out, far_lse,
     z_send, z_recv, y_send, y_recv, s_send, s_recv, q_send, q_recv, w_send, w_recv, own_sem,
 ):
@@ -80,13 +80,13 @@
             keys.at[SLOT[k_src], mine, at], keys.at[SLOT[k_dst], mine, at],
             z_send.at[way, step - 1, chunk], z_recv.at[way, step - 1, chunk], z_way[way])
 
-    def y_copy(k, which):
-        at = keys.at[SLOT[k], which]
-        return remote(at, at, y_send.at[k - 1], y_recv.at[k - 1], y_to)
-
-    def s_copy(k, row, which):
-        at = keys.at[SLOT[k], which]
-        return remote(at, at, s_send.at[row, k - 1], s_recv.at[row, k - 1], sibling)
+    def y_copy(k, which, chunk):
+        at = keys.at[SLOT[k], which, pl.ds(chunk * piece, piece)]
+        return remote(at, at, y_send.at[k - 1, chunk], y_recv.at[k - 1, chunk], y_to)
+
+    def s_copy(k, row, which, chunk):
+        at = keys.at[SLOT[k], which, pl.ds(chunk * piece, piece)]
+        return remote(at, at, s_send.at[row, k - 1, chunk], s_recv.at[row, k - 1, chunk], sibling)
 
     q_copy = remote(q_ref, q_far, q_send.at[0], q_recv.at[0], x_to)
     wv_copy = remote(wv_ref, wv_far, q_send.at[1], q_recv.at[1], x_to)
@@ -100,7 +100,8 @@
 
     for j in range(4):
         keys[0, j] = kv_ref[:, j * quarter:(j + 1) * quarter]
-    greet([*z_way, y_up, y_down, x_up, x_down, sibling])
+    greet([*z_way, y_up, y_down, device(x, y + 2, z, core), x_up, x_down, sibling,
+           device(x + 2, y, z, core), device(x + 2, y, z, 1 - core)])
 
     for chunk in (0, 1):
         for way in (0, 1):
@@ -174,26 +175,25 @@
                 z_copy(way, step, chunk).wait_recv()
                 if step < 3 or (step == 3 and chunk == way):
                     z_copy(way, step + 1, chunk).start()
-
-    def share_z(step):
-        for k in members[step]:
-            y_copy(k, mine).start()
-            s_copy(k, 0, mine).start()
+                k = step if way == 0 else 8 - step
+                y_copy(k, mine, chunk).start()
+                s_copy(k, 0, mine, chunk).start()
 
     def after_y(step):
-        for k in members[step]:
-            y_copy(k, other).wait_recv()
-            s_copy(k, 1, other).start()
+        for chunk in (0, 1):
+            for k in members[step]:
+                y_copy(k, other, chunk).wait_recv()
+                s_copy(k, 1, other, chunk).start()
 
     def after_s(step):
-        for k in members[step]:
-            s_copy(k, 0, sib_mine).wait_recv()
-            s_copy(k, 1, sib_other).wait_recv()
+        for chunk in (0, 1):
+            for k in members[step]:
+                s_copy(k, 0, sib_mine, chunk).wait_recv()
+                s_copy(k, 1, sib_other, chunk).wait_recv()
 
     tile(0, 0, 1, diagonal)
     after_z(1, 0)
     after_z(1, 1)
-    share_z(1)
 
     @pl.when(x_lo == 0)
     def _():
@@ -205,19 +205,16 @@
     after_y(1)
     far_tile(0, 1)
     after_z(2, 1)
-    share_z(2)
     after_s(1)
     own_pair(1)
     after_z(3, 0)
     after_y(2)
     far_tile(1, 2)
     after_z(3, 1)
-    share_z(3)
     after_s(2)
     own_pair(2)
     after_z(4, 0)
     after_z(4, 1)
-    share_z(4)
     after_y(3)
     far_tile(3, 2)
     after_s(3)
@@ -246,7 +243,7 @@
 
     @pl.when(x_lo == 0)
     def _():
-        out_ref[...] = head_out.astype(BF16)
+        heads[...] = head_out.astype(BF16).reshape(heads.shape)
 
     @pl.when(x_lo == 1)
     def _():
@@ -256,7 +253,8 @@
         far = jnp.broadcast_to(far_lse[0:1], (128, tokens)).T
         top = jnp.maximum(lse, far)
         near_part, far_part = jnp.exp2(lse - top), jnp.exp2(far - top)
-        out_ref[...] = ((head_out * near_part + far_out[...].astype(F32) * far_part) / (near_part + far_part)).astype(BF16)
+        merged = (head_out * near_part + far_out[...].astype(F32) * far_part) / (near_part + far_part)
+        heads[...] = merged.astype(BF16).reshape(heads.shape)
 
     wo_sib.wait_recv()
     wo_fwd.wait_recv()
@@ -269,9 +267,10 @@
                 if step < 4 or chunk == way:
                     z_copy(way, step, chunk).wait_send()
     for k in range(1, 8):
-        y_copy(k, mine).wait_send()
-        s_copy(k, 0, mine).wait_send()
-        s_copy(k, 1, other).wait_send()
+        for chunk in (0, 1):
+            y_copy(k, mine, chunk).wait_send()
+            s_copy(k, 0, mine, chunk).wait_send()
+            s_copy(k, 1, other, chunk).wait_send()
 
     @pl.when(x_lo == 1)
     def _():
@@ -282,40 +281,6 @@
     def _():
         back_copy.wait_send()
         lse_copy.wait_send()
-
-
-def attend(queries, kv, w_value, w_out):
-    width, tokens = queries.shape
-    latent, values = w_value.shape
-    dma = pltpu.SemaphoreType.DMA
-    vmem = pl.BlockSpec(memory_space=pltpu.VMEM)
-    hbm = pl.BlockSpec(memory_space=pl.ANY)
-    return pl.pallas_call(
-        attention_kernel,
-        out_shape=(
-            jax.ShapeDtypeStruct((tokens, values), BF16),
-            jax.ShapeDtypeStruct((4,) + w_out.shape, BF16),
-        ),
-        in_specs=[vmem, vmem, vmem, hbm],
-        out_specs=(vmem, hbm),
-        scratch_shapes=[
-            pltpu.VMEM((8, 4, width, tokens // 4), BF16),
-            pltpu.VMEM((width, tokens), BF16),
-            pltpu.VMEM((2, tokens, width), BF16),
-            pltpu.VMEM((latent, values), BF16),
-            pltpu.VMEM((2, tokens, 1), F32),
-            pltpu.VMEM((2, tokens, 1), F32),
-            pltpu.VMEM((2, tokens, latent), F32),
-            pltpu.VMEM((tokens, values), BF16),
-            pltpu.VMEM((8, tokens), F32),
-            pltpu.VMEM((tokens, values), BF16),
-            pltpu.VMEM((8, tokens), F32),
-            dma((2, 4, 2)), dma((2, 4, 2)), dma((7,)), dma((7,)), dma((2, 7)), dma((2, 7)),
-            dma((4,)), dma((4,)), dma((3,)), dma((3,)), dma,
-        ],
-        name="attention",
-        compiler_params=pltpu.CompilerParams(collective_id=0, has_side_effects=True, vmem_limit_bytes=56 << 20),
-    )(queries, kv, w_value, w_out)
 
 
 def routing_shares(ids_ref, scores_ref, experts):
@@ -330,11 +295,11 @@
     return jnp.where(lane < experts, coarse, dense - coarse).T
 
 
-def layer_kernel(
-    heads_ref, wo_ref, resid_ref, gain_ref, ids_ref, scores_ref, gate_ref, up_ref, down_ref, out_ref,
-    wo, gate, up, down, pool, proj, proj_out, y_in, after, rows_in, part, hidden, sib_in, x_out, x_in,
+def layer_part(
+    loads, heads_ref, wo, resid_ref, gain_ref, ids_ref, scores_ref, out_ref,
+    gate, up, down, pool, proj, proj_out, y_in, after, rows_in, part, hidden, sib_in, x_out, x_in,
     z_out, z_in,
-    load_sem, h_send, h_recv, y_send, y_recv, az_send, az_recv, ax_send, ax_recv, as_send, as_recv,
+    h_send, h_recv, y_send, y_recv, az_send, az_recv, ax_send, ax_recv, as_send, as_recv,
     bs_send, bs_recv, bx_send, bx_recv, bz_send, bz_recv,
 ):
     x, y, z, core = coords()
@@ -349,24 +314,15 @@
     across_sib = device(x + 2, y, z, 1 - core)
     y_at = [device(x, y + d, z, core) for d in (1, 2, 3)]
 
-    loads = [
-        pltpu.make_async_copy(src, dst, load_sem.at[i])
-        for i, (src, dst) in enumerate(((wo_ref, wo), (gate_ref, gate), (up_ref, up), (down_ref, down)))
-    ]
-    for load in loads:
-        load.start()
-
     mine = core * 2 + x_hi
     head_copies = [
         remote(heads_ref.at[c_to, :, x_to_hi], pool.at[mine], h_send.at[i], h_recv.at[i], target)
         for i, (c_to, x_to_hi, target) in enumerate((
             (1 - core, x_hi, sibling), (core, 1 - x_hi, across), (1 - core, 1 - x_hi, across_sib)))
     ]
-    greet([sibling, x_to, x_from, across, across_sib] + y_at + list(z_way))
     for copy in head_copies:
         copy.start()
     pool[mine] = heads_ref[core, :, x_hi]
-    loads[0].wait()
     for copy in head_copies:
         copy.wait_recv()
     features = jnp.concatenate([pool[i].reshape(4 * count, pool.shape[3]) for i in range(4)], axis=1)
@@ -398,12 +354,15 @@
             rows_in.at[SLOT[k_src], core, 0, at], rows_in.at[SLOT[k_dst], core, 0, at],
             az_send.at[way, step - 1, chunk], az_recv.at[way, step - 1, chunk], z_way[way])
 
-    def gather_x(k):
-        return remote(rows_in.at[SLOT[k], core, 0], rows_in.at[SLOT[k], core, 1], ax_send.at[k], ax_recv.at[k], x_to)
-
-    def gather_s(k, column, who):
-        at = rows_in.at[SLOT[k], who, column]
-        return remote(at, at, as_send.at[column, k], as_recv.at[column, k], sibling)
+    def gather_x(k, chunk):
+        at = pl.ds(chunk * piece, piece)
+        return remote(
+            rows_in.at[SLOT[k], core, 0, at], rows_in.at[SLOT[k], core, 1, at],
+            ax_send.at[k, chunk], ax_recv.at[k, chunk], x_to)
+
+    def gather_s(k, column, who, chunk):
+        at = rows_in.at[SLOT[k], who, column, pl.ds(chunk * piece, piece)]
+        return remote(at, at, as_send.at[column, k, chunk], as_recv.at[column, k, chunk], sibling)
 
     def return_s(slot, who):
         return remote(part.at[slot, who], sib_in.at[slot], bs_send.at[slot], bs_recv.at[slot], sibling)
@@ -451,50 +410,46 @@
                 gather_z(way, step, chunk).wait_recv()
                 if step < 3 or (step == 3 and chunk == way):
                     gather_z(way, step + 1, chunk).start()
-
-    def share_z(step):
-        for k in members[step]:
-            gather_x(k).start()
-            gather_s(k, 0, core).start()
+                k = step if way == 0 else 8 - step
+                gather_x(k, chunk).start()
+                gather_s(k, 0, core, chunk).start()
 
     def after_x(step):
-        for k in members[step]:
-            gather_x(k).wait_recv()
-            gather_s(k, 1, core).start()
+        for chunk in (0, 1):
+            for k in members[step]:
+                gather_x(k, chunk).wait_recv()
+                gather_s(k, 1, core, chunk).start()
 
     def after_s(step):
-        for k in members[step]:
-            gather_s(k, 0, 1 - core).wait_recv()
-            gather_s(k, 1, 1 - core).wait_recv()
+        for chunk in (0, 1):
+            for k in members[step]:
+                gather_s(k, 0, 1 - core, chunk).wait_recv()
+                gather_s(k, 1, 1 - core, chunk).wait_recv()
 
     for chunk in (0, 1):
         for way in (0, 1):
             gather_z(way, 1, chunk).start()
-    gather_x(0).start()
-    gather_s(0, 0, core).start()
-    for load in loads[1:]:
+        gather_x(0, chunk).start()
+        gather_s(0, 0, core, chunk).start()
+    for load in loads:
         load.wait()
     after_z(1, 0)
     after_z(1, 1)
-    share_z(1)
     after_x(0)
     after_s(0)
     hidden_units(0)
     after_z(2, 0)
     project_down(0)
     after_z(2, 1)
-    share_z(2)
     after_x(1)
     after_z(3, 0)
     after_s(1)
     fold_siblings(0)
     hidden_units(1)
     after_z(3, 1)
-    share_z(3)
     project_down(1)
     after_z(4, 0)
     after_z(4, 1)
-    share_z(4)
     after_x(2)
     after_s(2)
     hidden_units(2)
@@ -565,50 +520,90 @@
                 if step < 4 or chunk != way:
                     return_z(way, step if way == 1 else 8 - step, chunk).wait_send()
     for k in range(8):
-        gather_x(k).wait_send()
-        gather_s(k, 0, core).wait_send()
-        gather_s(k, 1, core).wait_send()
+        for chunk in (0, 1):
+            gather_x(k, chunk).wait_send()
+            gather_s(k, 0, core, chunk).wait_send()
+            gather_s(k, 1, core, chunk).wait_send()
         return_s(k, 1 - core).wait_send()
         return_x(k).wait_send()
 
 
-def finish_layer(head_out, w_out_part, resid, gain, ids, scores, gate, up, down):
-    count, width = resid.shape
-    units, values = gate.shape[0], head_out.shape[1]
-    heads = head_out.reshape(2, 4, 2, count, values)
+ATTENTION_SCRATCH = 22
+
+
+def layer_kernel(
+    q_ref, kv_ref, wv_ref, wo_ref, resid_ref, gain_ref, ids_ref, scores_ref, gate_ref, up_ref, down_ref, out_ref,
+    heads, wo, gate, up, down, load_sem, *scratch,
+):
+    loads = [
+        pltpu.make_async_copy(src, dst, load_sem.at[i])
+        for i, (src, dst) in enumerate(((gate_ref, gate), (up_ref, up), (down_ref, down)))
+    ]
+    for load in loads:
+        load.start()
+    attention_part(q_ref, kv_ref, wv_ref, wo_ref, heads, wo, *scratch[:ATTENTION_SCRATCH])
+    layer_part(
+        loads, heads, wo, resid_ref, gain_ref, ids_ref, scores_ref, out_ref,
+        gate, up, down, *scratch[ATTENTION_SCRATCH:])
+
+
+def run_layer(queries, kv, w_value, w_out, resid, gain, ids, scores, gate, up, down):
+    width, tokens = queries.shape
+    latent, values = w_value.shape
+    count, model = resid.shape
+    units = gate.shape[0]
     dma = pltpu.SemaphoreType.DMA
     vmem = pl.BlockSpec(memory_space=pltpu.VMEM)
     hbm = pl.BlockSpec(memory_space=pl.ANY)
+    attention_scratch = [
+        pltpu.VMEM((8, 4, width, tokens // 4), BF16),
+        pltpu.VMEM((width, tokens), BF16),
+        pltpu.VMEM((2, tokens, width), BF16),
+        pltpu.VMEM((latent, values), BF16),
+        pltpu.VMEM((2, tokens, 1), F32),
+        pltpu.VMEM((2, tokens, 1), F32),
+        pltpu.VMEM((2, tokens, latent), F32),
+        pltpu.VMEM((tokens, values), BF16),
+        pltpu.VMEM((8, tokens), F32),
+        pltpu.VMEM((tokens, values), BF16),
+        pltpu.VMEM((8, tokens), F32),
+        dma((2, 4, 2)), dma((2, 4, 2)), dma((7, 2)), dma((7, 2)), dma((2, 7, 2)), dma((2, 7, 2)),
+        dma((4,)), dma((4,)), dma((3,)), dma((3,)), dma,
+    ]
+    layer_scratch = [
+        pltpu.VMEM((4, 4, count, values), BF16),
+        pltpu.VMEM((4, count, model), F32),
+        pltpu.VMEM((4, count, model), BF16),
+        pltpu.VMEM((3, count, model), BF16),
+        pltpu.VMEM((count, model), BF16),
+        pltpu.VMEM((8, 2, 2, count, model + 128), BF16),
+        pltpu.VMEM((8, 2, 2, count, model), BF16),
+        pltpu.VMEM((8 * count, units), BF16),
+        pltpu.VMEM((8, 2, count, model), BF16),
+        pltpu.VMEM((8, count, model), BF16),
+        pltpu.VMEM((8, count, model), BF16),
+        pltpu.VMEM((2, 4, 2, count // 2, model), BF16),
+        pltpu.VMEM((2, 4, 2, count // 2, model), BF16),
+        dma((3,)), dma((3,)), dma((3,)), dma((3,)),
+        dma((2, 4, 2)), dma((2, 4, 2)), dma((8, 2)), dma((8, 2)), dma((2, 8, 2)), dma((2, 8, 2)),
+        dma((8,)), dma((8,)), dma((8,)), dma((8,)), dma((2, 4, 2)), dma((2, 4, 2)),
+    ]
     return pl.pallas_call(
         layer_kernel,
-        out_shape=jax.ShapeDtypeStruct((count, width), BF16),
-        in_specs=[vmem, hbm, vmem, vmem, vmem, vmem, hbm, hbm, hbm],
+        out_shape=jax.ShapeDtypeStruct((count, model), BF16),
+        in_specs=[vmem, vmem, vmem, hbm, vmem, vmem, vmem, vmem, hbm, hbm, hbm],
         out_specs=vmem,
         scratch_shapes=[
-            pltpu.VMEM(w_out_part.shape, BF16),
-            pltpu.VMEM((units, width), BF16),
-            pltpu.VMEM((units, width), BF16),
-            pltpu.VMEM((units, width), BF16),
-            pltpu.VMEM((4, 4, count, values), BF16),
-            pltpu.VMEM((4, count, width), F32),
-            pltpu.VMEM((4, count, width), BF16),
-            pltpu.VMEM((3, count, width), BF16),
-            pltpu.VMEM((count, width), BF16),
-            pltpu.VMEM((8, 2, 2, count, width + 128), BF16),
-            pltpu.VMEM((8, 2, 2, count, width), BF16),
-            pltpu.VMEM((8 * count, units), BF16),
-            pltpu.VMEM((8, 2, count, width), BF16),
-            pltpu.VMEM((8, count, width), BF16),
-            pltpu.VMEM((8, count, width), BF16),
-            pltpu.VMEM((2, 4, 2, count // 2, width), BF16),
-            pltpu.VMEM((2, 4, 2, count // 2, width), BF16),
-            dma((4,)), dma((3,)), dma((3,)), dma((3,)), dma((3,)),
-            dma((2, 4, 2)), dma((2, 4, 2)), dma((8,)), dma((8,)), dma((2, 8)), dma((2, 8)),
-            dma((8,)), dma((8,)), dma((8,)), dma((8,)), dma((2, 4, 2)), dma((2, 4, 2)),
-        ],
+            pltpu.VMEM((2, 4, 2, count, values), BF16),
+            pltpu.VMEM((4,) + w_out.shape, BF16),
+            pltpu.VMEM((units, model), BF16),
+            pltpu.VMEM((units, model), BF16),
+            pltpu.VMEM((units, model), BF16),
+            dma((3,)),
+        ] + attention_scratch + layer_scratch,
         name="layer",
-        compiler_params=pltpu.CompilerParams(collective_id=1, has_side_effects=True, vmem_limit_bytes=60 << 20),
-    )(heads, w_out_part, resid, gain.reshape(1, width), ids, scores, gate, up, down)
+        compiler_params=pltpu.CompilerParams(collective_id=0, has_side_effects=True, vmem_limit_bytes=60 << 20),
+    )(queries, kv, w_value, w_out, resid, gain.reshape(1, model), ids, scores, gate, up, down)
 
 
 def per_device(
@@ -624,11 +619,9 @@
     expert_ids,
     route_scores,
 ):
-    head_out, w_out_part = attend(
-        q_latent.reshape(q_latent.shape[0], q_latent.shape[2]).T, kv_latent.T, w_value[0], w_out
-    )
-    return finish_layer(
-        head_out, w_out_part, resid, norm_gain, expert_ids.T, route_scores.T, w_gate[0].T, w_up[0].T, w_down_t[0].T
+    return run_layer(
+        q_latent.reshape(q_latent.shape[0], q_latent.shape[2]).T, kv_latent.T, w_value[0], w_out,
+        resid, norm_gain, expert_ids.T, route_scores.T, w_gate[0].T, w_up[0].T, w_down_t[0].T,
     )
 
 

time: 123 us -> 118 us (0.959)
  Pallas kernels: 121 us -> 116 us
    pallas_call x2 -> x1, Pallas kernels: 121 us -> 116 us  [run_layer(): pl.pallas_call(layer_kernel, out_shape=jax.ShapeDtypeStruct((count, model...]
where the time goes in v4:
time: 118 us; the launch traced here: 117 us
  Pallas kernels  116 us (98%)
  local copies, waits for them, and re-layouts  1.57 us (1%)
    pallas_call x1, Pallas kernels, run_layer(): pl.pallas_call(layer_kernel, out_shape=jax.ShapeDtypeStruct((count, model...  116 us

profile of v4, /device:TPU:2, one launch (start us, length us, event | category | flops | bytes accessed | tf_op | source)
XLA Modules:
  0.0 117.4 jit_solution(11835401811488619535)
XLA Ops:
  0.0 115.8 %layer.1 = bf16[32,2048]{1,0:T(8,128)(2,1)} custom-call(bf16[576,512]{1,0:T(8,128)(2,1)} %bitcast.20, bf16[576,512]{1,0:T(8,128)(2,1)} %bitcast.21, bf16[512,128]{1,0:T(8,128)(2,1)} %bitcast.22, bf16[128,2048]{1,0:T(8,128)(2,1)} %wo_ref.1, bf16[32,2048]{1,0:T(8,128)(2,1)} %resid_ref.1, f32[1,2048]{1,0:T(1,128)} %bitcast.23, s32[6,32]{1,0:T(8,128)} %bitcast.24, ...), custom_call_target="tpu_custom_call" | custom-call | tf_op jit(solution)/shard_map/layer/pallas_call | solution.py:591
  115.8 1.6 %copy.13 = bf16[32,2048]{1,0:T(8,128)(2,1)} copy(bf16[32,2048]{1,0:T(8,128)(2,1)} %layer.1) | data formatting | bytes 262144

commit v5 on v4

--- a/solution.py
+++ b/solution.py
@@ -52,7 +52,7 @@
 
 
 def attention_part(
-    q_ref, kv_ref, wv_ref, wo_ref, heads, wo4_ref,
+    loads, q_ref, kv_ref, wv_ref, wo_ref, heads, wo4_ref,
     keys, q_far, queries, wv_far, high, denom, accum, back, back_lse, far_out, far_lse,
     z_send, z_recv, y_send, y_recv, s_send, s_recv, q_send, q_recv, w_send, w_recv, own_sem,
 ):
@@ -209,6 +209,8 @@
     own_pair(1)
     after_z(3, 0)
     after_y(2)
+    for load in loads:
+        load.start()
     far_tile(1, 2)
     after_z(3, 1)
     after_s(2)
@@ -216,12 +218,12 @@
     after_z(4, 0)
     after_z(4, 1)
     after_y(3)
+    wo_far.wait_recv()
+    wo_fwd.start()
     far_tile(3, 2)
     after_s(3)
     after_y(4)
     own_pair(3)
-    wo_far.wait_recv()
-    wo_fwd.start()
     far_tile(5, 2)
     after_s(4)
     far_tile(7, 1)
@@ -256,31 +258,36 @@
         merged = (head_out * near_part + far_out[...].astype(F32) * far_part) / (near_part + far_part)
         heads[...] = merged.astype(BF16).reshape(heads.shape)
 
-    wo_sib.wait_recv()
-    wo_fwd.wait_recv()
-    wo_own.wait()
-    for copy in (wo_sib, wo_far, wo_fwd):
-        copy.wait_send()
-    for step in range(1, 5):
-        for way in (0, 1):
+    def finish_waits():
+        for copy in (wo_sib, wo_far, wo_fwd):
+            copy.wait_send()
+        for step in range(1, 5):
+            for way in (0, 1):
+                for chunk in (0, 1):
+                    if step < 4 or chunk == way:
+                        z_copy(way, step, chunk).wait_send()
+        for k in range(1, 8):
             for chunk in (0, 1):
-                if step < 4 or chunk == way:
-                    z_copy(way, step, chunk).wait_send()
-    for k in range(1, 8):
-        for chunk in (0, 1):
-            y_copy(k, mine, chunk).wait_send()
-            s_copy(k, 0, mine, chunk).wait_send()
-            s_copy(k, 1, other, chunk).wait_send()
-
-    @pl.when(x_lo == 1)
-    def _():
-        q_copy.wait_send()
-        wv_copy.wait_send()
-
-    @pl.when(x_lo == 0)
-    def _():
-        back_copy.wait_send()
-        lse_copy.wait_send()
+                y_copy(k, mine, chunk).wait_send()
+                s_copy(k, 0, mine, chunk).wait_send()
+                s_copy(k, 1, other, chunk).wait_send()
+
+        @pl.when(x_lo == 1)
+        def _():
+            q_copy.wait_send()
+            wv_copy.wait_send()
+
+        @pl.when(x_lo == 0)
+        def _():
+            back_copy.wait_send()
+            lse_copy.wait_send()
+
+    def w_out_ready():
+        wo_sib.wait_recv()
+        wo_fwd.wait_recv()
+        wo_own.wait()
+
+    return w_out_ready, finish_waits
 
 
 def routing_shares(ids_ref, scores_ref, experts):
@@ -296,7 +303,7 @@
 
 
 def layer_part(
-    loads, heads_ref, wo, resid_ref, gain_ref, ids_ref, scores_ref, out_ref,
+    loads, w_out_ready, heads_ref, wo, resid_ref, gain_ref, ids_ref, scores_ref, out_ref,
     gate, up, down, pool, proj, proj_out, y_in, after, rows_in, part, hidden, sib_in, x_out, x_in,
     z_out, z_in,
     h_send, h_recv, y_send, y_recv, az_send, az_recv, ax_send, ax_recv, as_send, as_recv,
@@ -325,6 +332,7 @@
     pool[mine] = heads_ref[core, :, x_hi]
     for copy in head_copies:
         copy.wait_recv()
+    w_out_ready()
     features = jnp.concatenate([pool[i].reshape(4 * count, pool.shape[3]) for i in range(4)], axis=1)
     attended = dot(features, wo[...].reshape(features.shape[1], width)).reshape(4, count, width)
     proj[...] = attended
@@ -444,7 +452,6 @@
     after_x(1)
     after_z(3, 0)
     after_s(1)
-    fold_siblings(0)
     hidden_units(1)
     after_z(3, 1)
     project_down(1)
@@ -454,12 +461,10 @@
     after_s(2)
     hidden_units(2)
     after_x(3)
-    fold_siblings(1)
     project_down(2)
     after_s(3)
     hidden_units(3)
     after_x(4)
-    fold_siblings(2)
     project_down(3)
     after_s(4)
     hidden_units(4)
@@ -489,6 +494,8 @@
     pass_on(1, 3, 1, False)
     pass_on(0, 5, 0, False)
     fold_siblings(4)
+    for step in (2, 1, 0):
+        fold_siblings(step)
     settle(4)
     pass_on(1, 4, 0, False)
     pass_on(0, 4, 1, False)
@@ -539,12 +546,11 @@
         pltpu.make_async_copy(src, dst, load_sem.at[i])
         for i, (src, dst) in enumerate(((gate_ref, gate), (up_ref, up), (down_ref, down)))
     ]
-    for load in loads:
-        load.start()
-    attention_part(q_ref, kv_ref, wv_ref, wo_ref, heads, wo, *scratch[:ATTENTION_SCRATCH])
+    w_out_ready, finish_waits = attention_part(loads, q_ref, kv_ref, wv_ref, wo_ref, heads, wo, *scratch[:ATTENTION_SCRATCH])
     layer_part(
-        loads, heads, wo, resid_ref, gain_ref, ids_ref, scores_ref, out_ref,
+        loads, w_out_ready, heads, wo, resid_ref, gain_ref, ids_ref, scores_ref, out_ref,
         gate, up, down, *scratch[ATTENTION_SCRATCH:])
+    finish_waits()
 
 
 def run_layer(queries, kv, w_value, w_out, resid, gain, ids, scores, gate, up, down):

time: 118 us -> 118 us (level)
  no operation moved by 1% of the time
where the time goes in v5:
time: 118 us
  Pallas kernels  116 us (98%)
  local copies, waits for them, and re-layouts  1.57 us (1%)
    pallas_call x1, Pallas kernels, run_layer(): pl.pallas_call(layer_kernel, out_shape=jax.ShapeDtypeStruct((count, model...  116 us

profile of v5, /device:TPU:2, one launch (start us, length us, event | category | flops | bytes accessed | tf_op | source)
XLA Modules:
  0.0 117.8 jit_solution(17428255107086250588)
XLA Ops:
  0.0 116.3 %layer.1 = bf16[32,2048]{1,0:T(8,128)(2,1)} custom-call(bf16[576,512]{1,0:T(8,128)(2,1)} %bitcast.20, bf16[576,512]{1,0:T(8,128)(2,1)} %bitcast.21, bf16[512,128]{1,0:T(8,128)(2,1)} %bitcast.22, bf16[128,2048]{1,0:T(8,128)(2,1)} %wo_ref.1, bf16[32,2048]{1,0:T(8,128)(2,1)} %resid_ref.1, f32[1,2048]{1,0:T(1,128)} %bitcast.23, s32[6,32]{1,0:T(8,128)} %bitcast.24, ...), custom_call_target="tpu_custom_call" | custom-call | tf_op jit(solution)/shard_map/layer/pallas_call | solution.py:597
  116.3 1.6 %copy.13 = bf16[32,2048]{1,0:T(8,128)(2,1)} copy(bf16[32,2048]{1,0:T(8,128)(2,1)} %layer.1) | data formatting | bytes 262144
